TPU v7x, 512 devices: a whole 4x4x16 slice. The times are simulated.
512 devices in a mesh: lat: 64 (over y, z), lon: 8 (over x, core).
Axes of the slice: x: 4, y: 4, z: 16, core: 2. Of those that a mesh axis runs over, the one named last changes fastest.
Arguments:
- covariance: float32 [64, 64, 128, 128], P('lat', None, 'lon'), may hold values from -6 to 6
- winds: float32 [2, 3, 64, 128], P(None, None, None, 'lon'), may hold values from -0.35 to 0.35
- diffusivity: float32 [64, 128], P(None, 'lon'), may hold values from 0.01 to 0.07
- cutoff: int32 [64], replicated, may hold values from 4 to 16, as said below
Outputs:
- forecast: float32 [64, 64, 128, 128], P('lat', None, 'lon')
Inputs may be any that keep to these rules, and one draw needn't show every extreme that they name: Some latitude has cutoff 16 and some other has 4.
All inputs are finite; a program needn't handle non-finite values.
Results may differ from a plain program's by a relative error of at most 0.00002.
Values sent between devices are 32-bit elements; how exact they have to be, the bound alone decides.
A program may use at most 192 MiB of HBM per device.

v0:
```python
import jax
import jax.numpy as jnp
from jax import lax
from jax.sharding import PartitionSpec as P

STEPS = 3


def extended_2(block, sides, width):
    for axis, dim in sides:
        count = lax.axis_size(axis)
        forward = [(i, i + 1) for i in range(count - 1)]
        forward.append((count - 1, 0))
        backward = [(target, source) for source, target in forward]
        low = lax.ppermute(
            lax.slice_in_dim(block, block.shape[dim] - width, None, axis=dim), axis, forward
        )
        high = lax.ppermute(lax.slice_in_dim(block, 0, width, axis=dim), axis, backward)
        block = jnp.concatenate([low, block, high], axis=dim)
    return block


def from_behind(shard, axis, by):
    length = lax.axis_size(axis)
    pairs = [(i, i + by) for i in range(length) if 0 <= i + by < length]
    return lax.ppermute(shard, axis, pairs)


def advance(extended, east_wind, north_wind, spread):
    center = extended[:, :, 1:-1]
    western = extended[:, :, :-2]
    eastern = extended[:, :, 2:]
    zeros_row = jnp.zeros_like(center[:, :1])
    southern = jnp.concatenate([zeros_row, center[:, :-1]], axis=1)
    northern = jnp.concatenate([center[:, 1:], zeros_row], axis=1)
    east_wind = east_wind[None, :, :, None]
    north_wind = north_wind[None, :, :, None]
    spread = spread[None, :, :, None]
    transport = (
        jnp.maximum(east_wind, 0.0) * (center - western)
        + jnp.minimum(east_wind, 0.0) * (eastern - center)
        + jnp.maximum(north_wind, 0.0) * (center - southern)
        + jnp.minimum(north_wind, 0.0) * (northern - center)
    )
    return center - transport + spread * (eastern + western + northern + southern - 4.0 * center)


def propagate(state_field, winds, diffusivity):
    for substep in range(STEPS):
        extended = extended_2(state_field, (("lon", 2),), 1)
        state_field = advance(extended, winds[0, substep], winds[1, substep], diffusivity)
    return state_field


def relayout(block, reach_rows):
    row_count = block.shape[0]
    lat_count = block.shape[1]
    swapped = lax.all_to_all(block, "lon", split_axis=3, concat_axis=2, tiled=True)
    lon_count = swapped.shape[2]
    col_count = swapped.shape[3]
    block_count = lat_count // row_count
    device_index = lax.axis_index("lat")
    reach_blocks = min((reach_rows + row_count - 1) // row_count, block_count - 1)
    tile_blocks = swapped.reshape(row_count, block_count, row_count, lon_count, col_count)

    def piece_for(offset):
        target = jnp.clip(device_index + offset, 0, block_count - 1)
        return lax.dynamic_index_in_dim(tile_blocks, target, axis=1, keepdims=False)

    own_piece = piece_for(0)
    received = []
    for offset in range(-reach_blocks, reach_blocks + 1):
        if offset == 0:
            received.append(own_piece)
        else:
            received.append(from_behind(piece_for(offset), "lat", offset))
    window = jnp.stack(received[::-1], axis=0)
    padded = jnp.zeros(
        (block_count + 2 * reach_blocks, row_count, row_count, lon_count, col_count), jnp.float32
    )
    padded = lax.dynamic_update_slice_in_dim(padded, window, device_index, 0)
    regrouped = padded[reach_blocks : reach_blocks + block_count].reshape(
        lat_count, row_count, lon_count, col_count
    )
    return jnp.transpose(regrouped, (1, 0, 3, 2))


def per_device(covariance, winds, diffusivity, cutoff):
    row_count = covariance.shape[0]
    lat_count = covariance.shape[1]
    band_rows = lat_count // 4
    device_index = lax.axis_index("lat")
    lat_local = device_index * row_count + jnp.arange(row_count, dtype=jnp.int32)
    lat_all = jnp.arange(lat_count, dtype=jnp.int32)
    cut_local = lax.dynamic_slice_in_dim(cutoff, device_index * row_count, row_count)
    keep_first = jnp.abs(lat_all[None, :] - lat_local[:, None]) <= cutoff[None, :]
    keep_second = jnp.abs(lat_all[None, :] - lat_local[:, None]) <= cut_local[:, None]
    state_field = jnp.where(keep_first[:, :, None, None], covariance, 0.0)
    state_field = propagate(state_field, winds, diffusivity)
    state_field = relayout(state_field, band_rows + STEPS)
    state_field = propagate(state_field, winds, diffusivity)
    state_field = jnp.where(keep_second[:, :, None, None], state_field, 0.0)
    return relayout(state_field, band_rows)


def solution(mesh):
    in_specs = (P("lat", None, "lon", None), P(None, None, None, "lon"), P(None, "lon"), P())
    out_specs = P("lat", None, "lon", None)
    return jax.shard_map(
        per_device, mesh=mesh, in_specs=in_specs, out_specs=out_specs, check_vma=False
    )
```

profile of v0, /device:TPU:24, one launch (start us, length us, event | category | flops | bytes accessed | tf_op | source)
XLA Modules:
  0.0 880.4 jit_solution(16110254045664270610)
XLA Ops:
  2.5 2.9 collective-permute-start.1
  9.7 2.6 collective-permute-start.3
  16.1 3.0 collective-permute-start.5
  24.3 4.2 all-to-all-start
  28.5 10.3 %all-to-all-done = f32[8,1,16384]{2,1,0:T(1,128)S(1)} async-done(((f32[8,1,16384]{2,1,0:T(1,128)}), f32[8,1,16384]{2,1,0:T(1,128)S(1)}, u32[]{:S(2)}, u32[]{:S(2)}) %all-to-all-start) | async-done | bytes 524320 | tf_op jit(solution)/shard_map/all_to_all | solution.py:58
  44.4 8.4 constant_dynamic-slice_fusion.51
  54.4 21.2 %collective-permute-start.7 = (f32[1,1,128,16]{2,3,1,0:T(8,128)S(1)}, f32[1,1,128,16]{2,3,1,0:T(8,128)S(1)}, u32[]{:S(2)}, u32[]{:S(2)}) collective-permute-start(f32[1,1,128,16]{2,3,1,0:T(8,128)S(1)} %bitcast.330), channel_id=1, source_target_pairs={{0,144},{8,152},{16,160},{24,168},{32,176},{40,184},{48,192},{56,2... | collective-permute-start | bytes 24584 | tf_op jit(solution)/shard_map/ppermute | solution.py:26
  77.3 19.0 %collective-permute-start.8 = (f32[1,1,128,16]{2,3,1,0:T(8,128)S(1)}, f32[1,1,128,16]{2,3,1,0:T(8,128)S(1)}, u32[]{:S(2)}, u32[]{:S(2)}) collective-permute-start(f32[1,1,128,16]{2,3,1,0:T(8,128)S(1)} %bitcast.329), channel_id=1, source_target_pairs={{0,136},{8,144},{16,152},{24,160},{32,168},{40,176},{48,184},{56,1... | collective-permute-start | bytes 24584 | tf_op jit(solution)/shard_map/ppermute | solution.py:26
  100.8 8.6 collective-permute-start.10
  130.2 3.1 collective-permute-start.14
  139.1 4.8 collective-permute-start.18
  143.9 8.9 %constant_dynamic-slice_fusion.32 = (f32[1,1,1,128,16]{1,4,3,2,0:T(8,128)}, f32[1,1,1,128,16]{1,4,3,2,0:T(8,128)}, f32[1,1,1,128,16]{1,4,3,2,0:T(8,128)}, f32[1,...) fusion(f32[1,64,1,128,16]{1,4,3,2,0:T(8,128)S(1)} %bitcast.189,, ...), kind=kLoop, calls=%fused_computation.205 | loop fusion | bytes 294984 | tf_op jit(solution)/shard_map/jit(dynamic_index_in_dim)/dynamic_slice | solution.py:68
  197.3 2.5 collective-permute-start.22
  218.0 2.5 collective-permute-start.24
  222.6 6.4 collective-permute-start.26
  231.1 6.9 collective-permute-start.27
  239.4 7.8 collective-permute-start.28
  248.6 8.7 collective-permute-start.29
  263.3 2.3 constant_dynamic-update-slice_fusion.34
  270.2 2.4 constant_dynamic-update-slice_fusion.31
  272.5 2.3 constant_dynamic-update-slice_fusion.30
  292.9 2.3 constant_dynamic-update-slice_fusion.20
  295.2 10.0 %collective-permute-start.30 = (f32[1,1,128,16]{2,3,1,0:T(8,128)S(1)}, f32[1,1,128,16]{2,3,1,0:T(8,128)S(1)}, u32[]{:S(2)}, u32[]{:S(2)}) collective-permute-start(f32[1,1,128,16]{2,3,1,0:T(8,128)S(1)} %bitcast.218), channel_id=1, source_target_pairs={{48,0},{56,8},{64,16},{72,24},{80,32},{88,40},{96,48},{104,56},{11... | collective-permute-start | bytes 24584 | tf_op jit(solution)/shard_map/ppermute | solution.py:26
  305.7 11.5 %collective-permute-start.31 = (f32[1,1,128,16]{2,3,1,0:T(8,128)S(1)}, f32[1,1,128,16]{2,3,1,0:T(8,128)S(1)}, u32[]{:S(2)}, u32[]{:S(2)}) collective-permute-start(f32[1,1,128,16]{2,3,1,0:T(8,128)S(1)} %bitcast.217), channel_id=1, source_target_pairs={{56,0},{64,8},{72,16},{80,24},{88,32},{96,40},{104,48},{112,56},{1... | collective-permute-start | bytes 24584 | tf_op jit(solution)/shard_map/ppermute | solution.py:26
  317.2 12.4 %collective-permute-start.32 = (f32[1,1,128,16]{2,3,1,0:T(8,128)S(1)}, f32[1,1,128,16]{2,3,1,0:T(8,128)S(1)}, u32[]{:S(2)}, u32[]{:S(2)}) collective-permute-start(f32[1,1,128,16]{2,3,1,0:T(8,128)S(1)} %bitcast.216), channel_id=1, source_target_pairs={{64,0},{72,8},{80,16},{88,24},{96,32},{104,40},{112,48},{120,56},{... | collective-permute-start | bytes 24584 | tf_op jit(solution)/shard_map/ppermute | solution.py:26
  329.6 10.3 %collective-permute-start.33 = (f32[1,1,128,16]{2,3,1,0:T(8,128)S(1)}, f32[1,1,128,16]{2,3,1,0:T(8,128)S(1)}, u32[]{:S(2)}, u32[]{:S(2)}) collective-permute-start(f32[1,1,128,16]{2,3,1,0:T(8,128)S(1)} %bitcast.215), channel_id=1, source_target_pairs={{72,0},{80,8},{88,16},{96,24},{104,32},{112,40},{120,48},{128,56},... | collective-permute-start | bytes 24584 | tf_op jit(solution)/shard_map/ppermute | solution.py:26
  340.0 2.7 collective-permute-start.34
  357.7 13.2 %collective-permute-start.41 = (f32[1,1,128,16]{2,3,1,0:T(8,128)S(1)}, f32[1,1,128,16]{2,3,1,0:T(8,128)S(1)}, u32[]{:S(2)}, u32[]{:S(2)}) collective-permute-start(f32[1,1,128,16]{2,3,1,0:T(8,128)S(1)} %bitcast.199), channel_id=1, source_target_pairs={{136,0},{144,8},{152,16},{160,24},{168,32},{176,40},{184,48},{192,... | collective-permute-start | bytes 24584 | tf_op jit(solution)/shard_map/ppermute | solution.py:26
  371.0 19.0 %collective-permute-start.42 = (f32[1,1,128,16]{2,3,1,0:T(8,128)S(1)}, f32[1,1,128,16]{2,3,1,0:T(8,128)S(1)}, u32[]{:S(2)}, u32[]{:S(2)}) collective-permute-start(f32[1,1,128,16]{2,3,1,0:T(8,128)S(1)} %bitcast.198), channel_id=1, source_target_pairs={{144,0},{152,8},{160,16},{168,24},{176,32},{184,40},{192,48},{200,... | collective-permute-start | bytes 24584 | tf_op jit(solution)/shard_map/ppermute | solution.py:26
  390.0 19.0 %collective-permute-start.43 = (f32[1,1,128,16]{2,3,1,0:T(8,128)S(1)}, f32[1,1,128,16]{2,3,1,0:T(8,128)S(1)}, u32[]{:S(2)}, u32[]{:S(2)}) collective-permute-start(f32[1,1,128,16]{2,3,1,0:T(8,128)S(1)} %bitcast.197), channel_id=1, source_target_pairs={{152,0},{160,8},{168,16},{176,24},{184,32},{192,40},{200,48},{208,... | collective-permute-start | bytes 24584 | tf_op jit(solution)/shard_map/ppermute | solution.py:26
  409.0 9.1 %collective-permute-start.25 = (f32[1,1,128,16]{2,3,1,0:T(8,128)S(1)}, f32[1,1,128,16]{2,3,1,0:T(8,128)S(1)}, u32[]{:S(2)}, u32[]{:S(2)}) collective-permute-start(f32[1,1,128,16]{2,3,1,0:T(8,128)S(1)} %bitcast.265), channel_id=1, source_target_pairs={{8,0},{16,8},{24,16},{32,24},{40,32},{48,40},{56,48},{64,56},{72,6... | collective-permute-start | bytes 24584 | tf_op jit(solution)/shard_map/ppermute | solution.py:26
  447.5 2.4 constant_dynamic-update-slice_fusion.16
  449.9 2.3 constant_dynamic-update-slice_fusion.15
  480.4 2.3 constant_dynamic-update-slice_fusion
  482.8 23.8 %copy.588 = f32[39,1,1,128,16]{0,4,3,2,1:T(8,128)S(1)} copy(f32[39,1,1,128,16]{1,4,3,2,0:T(8,128)} %constant_dynamic-update-slice_fusion) | data formatting | bytes 638976 | tf_op jit(solution)/shard_map/stack | solution.py:77
  506.6 21.2 %dynamic_update_slice.6 = f32[102,1,1,128,16]{0,4,3,2,1:T(8,128)S(1)} dynamic-update-slice(f32[102,1,1,128,16]{0,4,3,2,1:T(8,128)S(1)} %broadcast_in_dim.38, f32[39,1,1,128,16]{0,4,3,2,1:T(8,128)S(1)} %copy.588, s32[]{:T(128)S(6)} %select_n.91, s32[]{:T(128)} %constant.241.clone.1, s32[]{:T(128)} %constant.241.clone.1, s32[]{:T(128)} %constant.241.clone.1, s32[]{:T(128)} %constant.241.clone.1) | dynamic-update-slice | bytes 638980 | tf_op jit(solution)/shard_map/dynamic_update_slice | solution.py:81
  528.3 2.9 collective-permute-start.45
  534.8 2.6 collective-permute-start.47
  540.5 3.0 collective-permute-start.49
  547.2 14.6 %all_to_all.30 = f32[8,1,16384]{2,1,0:T(1,128)S(1)} all-to-all(f32[8,1,16384]{2,1,0:T(1,128)S(1)} %reshape.178), channel_id=1, replica_groups=mesh['lat'=64,'lon'=8] {'lon'}, dimensions={0} | all-to-all | bytes 1048576 | tf_op jit(solution)/shard_map/all_to_all | solution.py:58
  564.6 7.4 constant_dynamic-slice_fusion.16
  576.6 2.9 collective-permute-start.51
  588.2 3.1 collective-permute-start.54
  608.8 4.4 collective-permute-start.59
  623.4 2.3 collective-permute-start.62
  629.8 2.7 collective-permute-start.65
  657.6 2.3 constant_dynamic-update-slice_fusion.66
  664.4 2.4 constant_dynamic-update-slice_fusion.63
  666.8 2.3 constant_dynamic-update-slice_fusion.62
  684.9 7.9 constant_dynamic-slice_fusion
  694.4 5.5 collective-permute-start.66
  701.5 4.8 collective-permute-start.67
  707.9 6.8 collective-permute-start.68
  716.4 7.4 collective-permute-start.69
  725.4 8.7 collective-permute-start.70
  735.8 12.0 %collective-permute-start.71 = (f32[1,1,128,16]{2,3,1,0:T(8,128)S(1)}, f32[1,1,128,16]{2,3,1,0:T(8,128)S(1)}, u32[]{:S(2)}, u32[]{:S(2)}) collective-permute-start(f32[1,1,128,16]{2,3,1,0:T(8,128)S(1)} %bitcast.320), channel_id=1, source_target_pairs={{48,0},{56,8},{64,16},{72,24},{80,32},{88,40},{96,48},{104,56},{11... | collective-permute-start | bytes 24584 | tf_op jit(solution)/shard_map/ppermute | solution.py:26
  755.9 9.7 %collective-permute-start.72 = (f32[1,1,128,16]{2,3,1,0:T(8,128)S(1)}, f32[1,1,128,16]{2,3,1,0:T(8,128)S(1)}, u32[]{:S(2)}, u32[]{:S(2)}) collective-permute-start(f32[1,1,128,16]{2,3,1,0:T(8,128)S(1)} %bitcast.311), channel_id=1, source_target_pairs={{56,0},{64,8},{72,16},{80,24},{88,32},{96,40},{104,48},{112,56},{1... | collective-permute-start | bytes 24584 | tf_op jit(solution)/shard_map/ppermute | solution.py:26
  765.6 12.4 %collective-permute-start.73 = (f32[1,1,128,16]{2,3,1,0:T(8,128)S(1)}, f32[1,1,128,16]{2,3,1,0:T(8,128)S(1)}, u32[]{:S(2)}, u32[]{:S(2)}) collective-permute-start(f32[1,1,128,16]{2,3,1,0:T(8,128)S(1)} %bitcast.304), channel_id=1, source_target_pairs={{64,0},{72,8},{80,16},{88,24},{96,32},{104,40},{112,48},{120,56},{... | collective-permute-start | bytes 24584 | tf_op jit(solution)/shard_map/ppermute | solution.py:26
  778.0 10.1 %collective-permute-start.74 = (f32[1,1,128,16]{2,3,1,0:T(8,128)S(1)}, f32[1,1,128,16]{2,3,1,0:T(8,128)S(1)}, u32[]{:S(2)}, u32[]{:S(2)}) collective-permute-start(f32[1,1,128,16]{2,3,1,0:T(8,128)S(1)} %bitcast.299), channel_id=1, source_target_pairs={{72,0},{80,8},{88,16},{96,24},{104,32},{112,40},{120,48},{128,56},... | collective-permute-start | bytes 24584 | tf_op jit(solution)/shard_map/ppermute | solution.py:26
  827.0 2.3 constant_dynamic-update-slice_fusion.53
  831.6 2.3 constant_dynamic-update-slice_fusion.51
  838.4 2.4 constant_dynamic-update-slice_fusion.48
  840.8 2.3 constant_dynamic-update-slice_fusion.47
  860.0 19.0 %copy.655 = f32[33,1,1,128,16]{3,4,0,2,1:T(8,128)S(1)} copy(f32[33,1,1,128,16]{1,4,3,2,0:T(8,128)} %constant_dynamic-update-slice_fusion.38) | data formatting | bytes 540672 | tf_op jit(solution)/shard_map/stack | solution.py:77
  (366 shorter events, 411.7 us)
Async XLA Ops:
  42.9 71.4 %collective-permute-start.6 = (f32[1,1,128,16]{2,3,1,0:T(8,128)S(1)}, f32[1,1,128,16]{2,3,1,0:T(8,128)S(1)}, u32[]{:S(2)}, u32[]{:S(2)}) collective-permute-start(f32[1,1,128,16]{2,3,1,0:T(8,128)S(1)} %bitcast.315), channel_id=1, source_target_pairs={{0,152},{8,160},{16,168},{24,176},{32,184},{40,192},{48,200},{56,2... | collective-permute-start | bytes 24584 | tf_op jit(solution)/shard_map/ppermute | solution.py:26
  54.4 61.8 %collective-permute-start.7 = (f32[1,1,128,16]{2,3,1,0:T(8,128)S(1)}, f32[1,1,128,16]{2,3,1,0:T(8,128)S(1)}, u32[]{:S(2)}, u32[]{:S(2)}) collective-permute-start(f32[1,1,128,16]{2,3,1,0:T(8,128)S(1)} %bitcast.330), channel_id=1, source_target_pairs={{0,144},{8,152},{16,160},{24,168},{32,176},{40,184},{48,192},{56,2... | collective-permute-start | bytes 24584 | tf_op jit(solution)/shard_map/ppermute | solution.py:26
  77.3 40.9 %collective-permute-start.8 = (f32[1,1,128,16]{2,3,1,0:T(8,128)S(1)}, f32[1,1,128,16]{2,3,1,0:T(8,128)S(1)}, u32[]{:S(2)}, u32[]{:S(2)}) collective-permute-start(f32[1,1,128,16]{2,3,1,0:T(8,128)S(1)} %bitcast.329), channel_id=1, source_target_pairs={{0,136},{8,144},{16,152},{24,160},{32,168},{40,176},{48,184},{56,1... | collective-permute-start | bytes 24584 | tf_op jit(solution)/shard_map/ppermute | solution.py:26
  97.9 32.3 %collective-permute-start.9 = (f32[1,1,128,16]{2,3,1,0:T(8,128)S(1)}, f32[1,1,128,16]{2,3,1,0:T(8,128)S(1)}, u32[]{:S(2)}, u32[]{:S(2)}) collective-permute-start(f32[1,1,128,16]{2,3,1,0:T(8,128)S(1)} %bitcast.232), channel_id=1, source_target_pairs={{0,128},{8,136},{16,144},{24,152},{32,160},{40,168},{48,176},{56,1... | collective-permute-start | bytes 24584 | tf_op jit(solution)/shard_map/ppermute | solution.py:26
  100.8 32.5 %collective-permute-start.10 = (f32[1,1,128,16]{2,3,1,0:T(8,128)S(1)}, f32[1,1,128,16]{2,3,1,0:T(8,128)S(1)}, u32[]{:S(2)}, u32[]{:S(2)}) collective-permute-start(f32[1,1,128,16]{2,3,1,0:T(8,128)S(1)} %bitcast.231), channel_id=1, source_target_pairs={{0,120},{8,128},{16,136},{24,144},{32,152},{40,160},{48,168},{56,1... | collective-permute-start | bytes 24584 | tf_op jit(solution)/shard_map/ppermute | solution.py:26
  114.3 20.9 %collective-permute-start.11 = (f32[1,1,128,16]{2,3,1,0:T(8,128)S(1)}, f32[1,1,128,16]{2,3,1,0:T(8,128)S(1)}, u32[]{:S(2)}, u32[]{:S(2)}) collective-permute-start(f32[1,1,128,16]{2,3,1,0:T(8,128)S(1)} %bitcast.230), channel_id=1, source_target_pairs={{0,112},{8,120},{16,128},{24,136},{32,144},{40,152},{48,160},{56,1... | collective-permute-start | bytes 24584 | tf_op jit(solution)/shard_map/ppermute | solution.py:26
  116.3 20.9 %collective-permute-start.12 = (f32[1,1,128,16]{2,3,1,0:T(8,128)S(1)}, f32[1,1,128,16]{2,3,1,0:T(8,128)S(1)}, u32[]{:S(2)}, u32[]{:S(2)}) collective-permute-start(f32[1,1,128,16]{2,3,1,0:T(8,128)S(1)} %bitcast.229), channel_id=1, source_target_pairs={{0,104},{8,112},{16,120},{24,128},{32,136},{40,144},{48,152},{56,1... | collective-permute-start | bytes 24584 | tf_op jit(solution)/shard_map/ppermute | solution.py:26
  118.2 20.9 %collective-permute-start.13 = (f32[1,1,128,16]{2,3,1,0:T(8,128)S(1)}, f32[1,1,128,16]{2,3,1,0:T(8,128)S(1)}, u32[]{:S(2)}, u32[]{:S(2)}) collective-permute-start(f32[1,1,128,16]{2,3,1,0:T(8,128)S(1)} %bitcast.228), channel_id=1, source_target_pairs={{0,96},{8,104},{16,112},{24,120},{32,128},{40,136},{48,144},{56,15... | collective-permute-start | bytes 24584 | tf_op jit(solution)/shard_map/ppermute | solution.py:26
  130.2 61.2 %collective-permute-start.14 = (f32[1,1,128,16]{2,3,1,0:T(8,128)}, f32[1,1,128,16]{2,3,1,0:T(8,128)S(1)}, u32[]{:S(2)}, u32[]{:S(2)}) collective-permute-start(f32[1,1,128,16]{2,3,1,0:T(8,128)} %bitcast.32), channel_id=1, source_target_pairs={{0,88},{8,96},{16,104},{24,112},{32,120},{40,128},{48,136},{56,144... | collective-permute-start | bytes 24584 | tf_op jit(solution)/shard_map/ppermute | solution.py:26
  133.3 60.1 %collective-permute-start.15 = (f32[1,1,128,16]{2,3,1,0:T(8,128)}, f32[1,1,128,16]{2,3,1,0:T(8,128)S(1)}, u32[]{:S(2)}, u32[]{:S(2)}) collective-permute-start(f32[1,1,128,16]{2,3,1,0:T(8,128)} %bitcast.34), channel_id=1, source_target_pairs={{0,80},{8,88},{16,96},{24,104},{32,112},{40,120},{48,128},{56,136}... | collective-permute-start | bytes 24584 | tf_op jit(solution)/shard_map/ppermute | solution.py:26
  135.2 60.1 %collective-permute-start.16 = (f32[1,1,128,16]{2,3,1,0:T(8,128)S(1)}, f32[1,1,128,16]{2,3,1,0:T(8,128)S(1)}, u32[]{:S(2)}, u32[]{:S(2)}) collective-permute-start(f32[1,1,128,16]{2,3,1,0:T(8,128)S(1)} %bitcast.245), channel_id=1, source_target_pairs={{0,72},{8,80},{16,88},{24,96},{32,104},{40,112},{48,120},{56,128},... | collective-permute-start | bytes 24584 | tf_op jit(solution)/shard_map/ppermute | solution.py:26
  137.2 60.1 %collective-permute-start.17 = (f32[1,1,128,16]{2,3,1,0:T(8,128)S(1)}, f32[1,1,128,16]{2,3,1,0:T(8,128)S(1)}, u32[]{:S(2)}, u32[]{:S(2)}) collective-permute-start(f32[1,1,128,16]{2,3,1,0:T(8,128)S(1)} %bitcast.239), channel_id=1, source_target_pairs={{0,64},{8,72},{16,80},{24,88},{32,96},{40,104},{48,112},{56,120},{... | collective-permute-start | bytes 24584 | tf_op jit(solution)/shard_map/ppermute | solution.py:26
  139.1 60.7 %collective-permute-start.18 = (f32[1,1,128,16]{2,3,1,0:T(8,128)S(1)}, f32[1,1,128,16]{2,3,1,0:T(8,128)S(1)}, u32[]{:S(2)}, u32[]{:S(2)}) collective-permute-start(f32[1,1,128,16]{2,3,1,0:T(8,128)S(1)} %bitcast.237), channel_id=1, source_target_pairs={{0,56},{8,64},{16,72},{24,80},{32,88},{40,96},{48,104},{56,112},{6... | collective-permute-start | bytes 24584 | tf_op jit(solution)/shard_map/ppermute | solution.py:26
  191.3 26.6 %collective-permute-start.19 = (f32[1,1,128,16]{2,3,1,0:T(8,128)}, f32[1,1,128,16]{2,3,1,0:T(8,128)}, u32[]{:S(2)}, u32[]{:S(2)}) collective-permute-start(f32[1,1,128,16]{2,3,1,0:T(8,128)} %bitcast.258), channel_id=1, source_target_pairs={{0,48},{8,56},{16,64},{24,72},{32,80},{40,88},{48,96},{56,104},{64... | collective-permute-start | bytes 24584 | tf_op jit(solution)/shard_map/ppermute | solution.py:26
  193.4 29.1 %collective-permute-start.20 = (f32[1,1,128,16]{2,3,1,0:T(8,128)}, f32[1,1,128,16]{2,3,1,0:T(8,128)}, u32[]{:S(2)}, u32[]{:S(2)}) collective-permute-start(f32[1,1,128,16]{2,3,1,0:T(8,128)} %bitcast.253), channel_id=1, source_target_pairs={{0,40},{8,48},{16,56},{24,64},{32,72},{40,80},{48,88},{56,96},{64,... | collective-permute-start | bytes 24584 | tf_op jit(solution)/shard_map/ppermute | solution.py:26
  195.4 35.7 %collective-permute-start.21 = (f32[1,1,128,16]{2,3,1,0:T(8,128)S(1)}, f32[1,1,128,16]{2,3,1,0:T(8,128)S(1)}, u32[]{:S(2)}, u32[]{:S(2)}) collective-permute-start(f32[1,1,128,16]{2,3,1,0:T(8,128)S(1)} %bitcast.247), channel_id=1, source_target_pairs={{0,32},{8,40},{16,48},{24,56},{32,64},{40,72},{48,80},{56,88},{64,... | collective-permute-start | bytes 24584 | tf_op jit(solution)/shard_map/ppermute | solution.py:26
  197.3 42.1 %collective-permute-start.22 = (f32[1,1,128,16]{2,3,1,0:T(8,128)S(1)}, f32[1,1,128,16]{2,3,1,0:T(8,128)S(1)}, u32[]{:S(2)}, u32[]{:S(2)}) collective-permute-start(f32[1,1,128,16]{2,3,1,0:T(8,128)S(1)} %bitcast.240), channel_id=1, source_target_pairs={{0,24},{8,32},{16,40},{24,48},{32,56},{40,64},{48,72},{56,80},{64,... | collective-permute-start | bytes 24584 | tf_op jit(solution)/shard_map/ppermute | solution.py:26
  199.8 48.8 %collective-permute-start.23 = (f32[1,1,128,16]{2,3,1,0:T(8,128)S(1)}, f32[1,1,128,16]{2,3,1,0:T(8,128)S(1)}, u32[]{:S(2)}, u32[]{:S(2)}) collective-permute-start(f32[1,1,128,16]{2,3,1,0:T(8,128)S(1)} %bitcast.236), channel_id=1, source_target_pairs={{0,16},{8,24},{16,32},{24,40},{32,48},{40,56},{48,64},{56,72},{64,... | collective-permute-start | bytes 24584 | tf_op jit(solution)/shard_map/ppermute | solution.py:26
  218.0 77.2 %collective-permute-start.24 = (f32[1,1,128,16]{2,3,1,0:T(8,128)S(1)}, f32[1,1,128,16]{2,3,1,0:T(8,128)S(1)}, u32[]{:S(2)}, u32[]{:S(2)}) collective-permute-start(f32[1,1,128,16]{2,3,1,0:T(8,128)S(1)} %bitcast.225), channel_id=1, source_target_pairs={{0,8},{8,16},{16,24},{24,32},{32,40},{40,48},{48,56},{56,64},{64,7... | collective-permute-start | bytes 24584 | tf_op jit(solution)/shard_map/ppermute | solution.py:26
  222.6 83.2 %collective-permute-start.26 = (f32[1,1,128,16]{2,3,1,0:T(8,128)S(1)}, f32[1,1,128,16]{2,3,1,0:T(8,128)S(1)}, u32[]{:S(2)}, u32[]{:S(2)}) collective-permute-start(f32[1,1,128,16]{2,3,1,0:T(8,128)S(1)} %bitcast.223), channel_id=1, source_target_pairs={{16,0},{24,8},{32,16},{40,24},{48,32},{56,40},{64,48},{72,56},{80,... | collective-permute-start | bytes 24584 | tf_op jit(solution)/shard_map/ppermute | solution.py:26
  231.1 86.1 %collective-permute-start.27 = (f32[1,1,128,16]{2,3,1,0:T(8,128)S(1)}, f32[1,1,128,16]{2,3,1,0:T(8,128)S(1)}, u32[]{:S(2)}, u32[]{:S(2)}) collective-permute-start(f32[1,1,128,16]{2,3,1,0:T(8,128)S(1)} %bitcast.222), channel_id=1, source_target_pairs={{24,0},{32,8},{40,16},{48,24},{56,32},{64,40},{72,48},{80,56},{88,... | collective-permute-start | bytes 24584 | tf_op jit(solution)/shard_map/ppermute | solution.py:26
  239.4 90.2 %collective-permute-start.28 = (f32[1,1,128,16]{2,3,1,0:T(8,128)S(1)}, f32[1,1,128,16]{2,3,1,0:T(8,128)S(1)}, u32[]{:S(2)}, u32[]{:S(2)}) collective-permute-start(f32[1,1,128,16]{2,3,1,0:T(8,128)S(1)} %bitcast.220), channel_id=1, source_target_pairs={{32,0},{40,8},{48,16},{56,24},{64,32},{72,40},{80,48},{88,56},{96,... | collective-permute-start | bytes 24584 | tf_op jit(solution)/shard_map/ppermute | solution.py:26
  248.6 91.3 %collective-permute-start.29 = (f32[1,1,128,16]{2,3,1,0:T(8,128)S(1)}, f32[1,1,128,16]{2,3,1,0:T(8,128)S(1)}, u32[]{:S(2)}, u32[]{:S(2)}) collective-permute-start(f32[1,1,128,16]{2,3,1,0:T(8,128)S(1)} %bitcast.219), channel_id=1, source_target_pairs={{40,0},{48,8},{56,16},{64,24},{72,32},{80,40},{88,48},{96,56},{104... | collective-permute-start | bytes 24584 | tf_op jit(solution)/shard_map/ppermute | solution.py:26
  295.2 48.5 %collective-permute-start.30 = (f32[1,1,128,16]{2,3,1,0:T(8,128)S(1)}, f32[1,1,128,16]{2,3,1,0:T(8,128)S(1)}, u32[]{:S(2)}, u32[]{:S(2)}) collective-permute-start(f32[1,1,128,16]{2,3,1,0:T(8,128)S(1)} %bitcast.218), channel_id=1, source_target_pairs={{48,0},{56,8},{64,16},{72,24},{80,32},{88,40},{96,48},{104,56},{11... | collective-permute-start | bytes 24584 | tf_op jit(solution)/shard_map/ppermute | solution.py:26
  305.7 39.9 %collective-permute-start.31 = (f32[1,1,128,16]{2,3,1,0:T(8,128)S(1)}, f32[1,1,128,16]{2,3,1,0:T(8,128)S(1)}, u32[]{:S(2)}, u32[]{:S(2)}) collective-permute-start(f32[1,1,128,16]{2,3,1,0:T(8,128)S(1)} %bitcast.217), channel_id=1, source_target_pairs={{56,0},{64,8},{72,16},{80,24},{88,32},{96,40},{104,48},{112,56},{1... | collective-permute-start | bytes 24584 | tf_op jit(solution)/shard_map/ppermute | solution.py:26
  317.2 30.4 %collective-permute-start.32 = (f32[1,1,128,16]{2,3,1,0:T(8,128)S(1)}, f32[1,1,128,16]{2,3,1,0:T(8,128)S(1)}, u32[]{:S(2)}, u32[]{:S(2)}) collective-permute-start(f32[1,1,128,16]{2,3,1,0:T(8,128)S(1)} %bitcast.216), channel_id=1, source_target_pairs={{64,0},{72,8},{80,16},{88,24},{96,32},{104,40},{112,48},{120,56},{... | collective-permute-start | bytes 24584 | tf_op jit(solution)/shard_map/ppermute | solution.py:26
  329.6 19.9 %collective-permute-start.33 = (f32[1,1,128,16]{2,3,1,0:T(8,128)S(1)}, f32[1,1,128,16]{2,3,1,0:T(8,128)S(1)}, u32[]{:S(2)}, u32[]{:S(2)}) collective-permute-start(f32[1,1,128,16]{2,3,1,0:T(8,128)S(1)} %bitcast.215), channel_id=1, source_target_pairs={{72,0},{80,8},{88,16},{96,24},{104,32},{112,40},{120,48},{128,56},... | collective-permute-start | bytes 24584 | tf_op jit(solution)/shard_map/ppermute | solution.py:26
  347.6 23.4 %collective-permute-start.37 = (f32[1,1,128,16]{2,3,1,0:T(8,128)S(1)}, f32[1,1,128,16]{2,3,1,0:T(8,128)S(1)}, u32[]{:S(2)}, u32[]{:S(2)}) collective-permute-start(f32[1,1,128,16]{2,3,1,0:T(8,128)S(1)} %bitcast.211), channel_id=1, source_target_pairs={{104,0},{112,8},{120,16},{128,24},{136,32},{144,40},{152,48},{160,... | collective-permute-start | bytes 24584 | tf_op jit(solution)/shard_map/ppermute | solution.py:26
  349.5 40.5 %collective-permute-start.38 = (f32[1,1,128,16]{2,3,1,0:T(8,128)S(1)}, f32[1,1,128,16]{2,3,1,0:T(8,128)S(1)}, u32[]{:S(2)}, u32[]{:S(2)}) collective-permute-start(f32[1,1,128,16]{2,3,1,0:T(8,128)S(1)} %bitcast.210), channel_id=1, source_target_pairs={{112,0},{120,8},{128,16},{136,24},{144,32},{152,40},{160,48},{168,... | collective-permute-start | bytes 24584 | tf_op jit(solution)/shard_map/ppermute | solution.py:26
  352.4 56.6 %collective-permute-start.39 = (f32[1,1,128,16]{2,3,1,0:T(8,128)S(1)}, f32[1,1,128,16]{2,3,1,0:T(8,128)S(1)}, u32[]{:S(2)}, u32[]{:S(2)}) collective-permute-start(f32[1,1,128,16]{2,3,1,0:T(8,128)S(1)} %bitcast.209), channel_id=1, source_target_pairs={{120,0},{128,8},{136,16},{144,24},{152,32},{160,40},{168,48},{176,... | collective-permute-start | bytes 24584 | tf_op jit(solution)/shard_map/ppermute | solution.py:26
  356.4 79.4 %collective-permute-start.40 = (f32[1,1,128,16]{2,3,1,0:T(8,128)S(1)}, f32[1,1,128,16]{2,3,1,0:T(8,128)S(1)}, u32[]{:S(2)}, u32[]{:S(2)}) collective-permute-start(f32[1,1,128,16]{2,3,1,0:T(8,128)S(1)} %bitcast.200), channel_id=1, source_target_pairs={{128,0},{136,8},{144,16},{152,24},{160,32},{168,40},{176,48},{184,... | collective-permute-start | bytes 24584 | tf_op jit(solution)/shard_map/ppermute | solution.py:26
  357.7 79.6 %collective-permute-start.41 = (f32[1,1,128,16]{2,3,1,0:T(8,128)S(1)}, f32[1,1,128,16]{2,3,1,0:T(8,128)S(1)}, u32[]{:S(2)}, u32[]{:S(2)}) collective-permute-start(f32[1,1,128,16]{2,3,1,0:T(8,128)S(1)} %bitcast.199), channel_id=1, source_target_pairs={{136,0},{144,8},{152,16},{160,24},{168,32},{176,40},{184,48},{192,... | collective-permute-start | bytes 24584 | tf_op jit(solution)/shard_map/ppermute | solution.py:26
  371.0 67.7 %collective-permute-start.42 = (f32[1,1,128,16]{2,3,1,0:T(8,128)S(1)}, f32[1,1,128,16]{2,3,1,0:T(8,128)S(1)}, u32[]{:S(2)}, u32[]{:S(2)}) collective-permute-start(f32[1,1,128,16]{2,3,1,0:T(8,128)S(1)} %bitcast.198), channel_id=1, source_target_pairs={{144,0},{152,8},{160,16},{168,24},{176,32},{184,40},{192,48},{200,... | collective-permute-start | bytes 24584 | tf_op jit(solution)/shard_map/ppermute | solution.py:26
  390.0 50.1 %collective-permute-start.43 = (f32[1,1,128,16]{2,3,1,0:T(8,128)S(1)}, f32[1,1,128,16]{2,3,1,0:T(8,128)S(1)}, u32[]{:S(2)}, u32[]{:S(2)}) collective-permute-start(f32[1,1,128,16]{2,3,1,0:T(8,128)S(1)} %bitcast.197), channel_id=1, source_target_pairs={{152,0},{160,8},{168,16},{176,24},{184,32},{192,40},{200,48},{208,... | collective-permute-start | bytes 24584 | tf_op jit(solution)/shard_map/ppermute | solution.py:26
  409.0 32.5 %collective-permute-start.25 = (f32[1,1,128,16]{2,3,1,0:T(8,128)S(1)}, f32[1,1,128,16]{2,3,1,0:T(8,128)S(1)}, u32[]{:S(2)}, u32[]{:S(2)}) collective-permute-start(f32[1,1,128,16]{2,3,1,0:T(8,128)S(1)} %bitcast.265), channel_id=1, source_target_pairs={{8,0},{16,8},{24,16},{32,24},{40,32},{48,40},{56,48},{64,56},{72,6... | collective-permute-start | bytes 24584 | tf_op jit(solution)/shard_map/ppermute | solution.py:26
  573.6 19.3 %collective-permute-start.50 = (f32[1,1,128,16]{2,3,1,0:T(8,128)S(1)}, f32[1,1,128,16]{2,3,1,0:T(8,128)S(1)}, u32[]{:S(2)}, u32[]{:S(2)}) collective-permute-start(f32[1,1,128,16]{2,3,1,0:T(8,128)S(1)} %bitcast.331), channel_id=1, source_target_pairs={{0,128},{8,136},{16,144},{24,152},{32,160},{40,168},{48,176},{56,1... | collective-permute-start | bytes 24584 | tf_op jit(solution)/shard_map/ppermute | solution.py:26
  576.6 26.4 %collective-permute-start.51 = (f32[1,1,128,16]{2,3,1,0:T(8,128)S(1)}, f32[1,1,128,16]{2,3,1,0:T(8,128)S(1)}, u32[]{:S(2)}, u32[]{:S(2)}) collective-permute-start(f32[1,1,128,16]{2,3,1,0:T(8,128)S(1)} %bitcast.327), channel_id=1, source_target_pairs={{0,120},{8,128},{16,136},{24,144},{32,152},{40,160},{48,168},{56,1... | collective-permute-start | bytes 24584 | tf_op jit(solution)/shard_map/ppermute | solution.py:26
  581.1 23.9 %collective-permute-start.52 = (f32[1,1,128,16]{2,3,1,0:T(8,128)S(1)}, f32[1,1,128,16]{2,3,1,0:T(8,128)S(1)}, u32[]{:S(2)}, u32[]{:S(2)}) collective-permute-start(f32[1,1,128,16]{2,3,1,0:T(8,128)S(1)} %bitcast.325), channel_id=1, source_target_pairs={{0,112},{8,120},{16,128},{24,136},{32,144},{40,152},{48,160},{56,1... | collective-permute-start | bytes 24584 | tf_op jit(solution)/shard_map/ppermute | solution.py:26
  584.6 22.3 %collective-permute-start.53 = (f32[1,1,128,16]{2,3,1,0:T(8,128)S(1)}, f32[1,1,128,16]{2,3,1,0:T(8,128)S(1)}, u32[]{:S(2)}, u32[]{:S(2)}) collective-permute-start(f32[1,1,128,16]{2,3,1,0:T(8,128)S(1)} %bitcast.323), channel_id=1, source_target_pairs={{0,104},{8,112},{16,120},{24,128},{32,136},{40,144},{48,152},{56,1... | collective-permute-start | bytes 24584 | tf_op jit(solution)/shard_map/ppermute | solution.py:26
  588.2 20.6 %collective-permute-start.54 = (f32[1,1,128,16]{2,3,1,0:T(8,128)S(1)}, f32[1,1,128,16]{2,3,1,0:T(8,128)S(1)}, u32[]{:S(2)}, u32[]{:S(2)}) collective-permute-start(f32[1,1,128,16]{2,3,1,0:T(8,128)S(1)} %bitcast.321), channel_id=1, source_target_pairs={{0,96},{8,104},{16,112},{24,120},{32,128},{40,136},{48,144},{56,15... | collective-permute-start | bytes 24584 | tf_op jit(solution)/shard_map/ppermute | solution.py:26
  592.9 20.3 %collective-permute-start.55 = (f32[1,1,128,16]{2,3,1,0:T(8,128)S(1)}, f32[1,1,128,16]{2,3,1,0:T(8,128)S(1)}, u32[]{:S(2)}, u32[]{:S(2)}) collective-permute-start(f32[1,1,128,16]{2,3,1,0:T(8,128)S(1)} %bitcast.318), channel_id=1, source_target_pairs={{0,88},{8,96},{16,104},{24,112},{32,120},{40,128},{48,136},{56,144... | collective-permute-start | bytes 24584 | tf_op jit(solution)/shard_map/ppermute | solution.py:26
  603.0 18.4 %collective-permute-start.56 = (f32[1,1,128,16]{2,3,1,0:T(8,128)S(1)}, f32[1,1,128,16]{2,3,1,0:T(8,128)S(1)}, u32[]{:S(2)}, u32[]{:S(2)}) collective-permute-start(f32[1,1,128,16]{2,3,1,0:T(8,128)S(1)} %bitcast.308), channel_id=1, source_target_pairs={{0,80},{8,88},{16,96},{24,104},{32,112},{40,120},{48,128},{56,136}... | collective-permute-start | bytes 24584 | tf_op jit(solution)/shard_map/ppermute | solution.py:26
  604.9 18.4 %collective-permute-start.57 = (f32[1,1,128,16]{2,3,1,0:T(8,128)S(1)}, f32[1,1,128,16]{2,3,1,0:T(8,128)S(1)}, u32[]{:S(2)}, u32[]{:S(2)}) collective-permute-start(f32[1,1,128,16]{2,3,1,0:T(8,128)S(1)} %bitcast.301), channel_id=1, source_target_pairs={{0,72},{8,80},{16,88},{24,96},{32,104},{40,112},{48,120},{56,128},... | collective-permute-start | bytes 24584 | tf_op jit(solution)/shard_map/ppermute | solution.py:26
  606.9 18.8 %collective-permute-start.58 = (f32[1,1,128,16]{2,3,1,0:T(8,128)S(1)}, f32[1,1,128,16]{2,3,1,0:T(8,128)S(1)}, u32[]{:S(2)}, u32[]{:S(2)}) collective-permute-start(f32[1,1,128,16]{2,3,1,0:T(8,128)S(1)} %bitcast.293), channel_id=1, source_target_pairs={{0,64},{8,72},{16,80},{24,88},{32,96},{40,104},{48,112},{56,120},{... | collective-permute-start | bytes 24584 | tf_op jit(solution)/shard_map/ppermute | solution.py:26
  608.8 19.0 %collective-permute-start.59 = (f32[1,1,128,16]{2,3,1,0:T(8,128)S(1)}, f32[1,1,128,16]{2,3,1,0:T(8,128)S(1)}, u32[]{:S(2)}, u32[]{:S(2)}) collective-permute-start(f32[1,1,128,16]{2,3,1,0:T(8,128)S(1)} %bitcast.286), channel_id=1, source_target_pairs={{0,56},{8,64},{16,72},{24,80},{32,88},{40,96},{48,104},{56,112},{6... | collective-permute-start | bytes 24584 | tf_op jit(solution)/shard_map/ppermute | solution.py:26
  621.5 24.4 %collective-permute-start.61 = (f32[1,1,128,16]{2,3,1,0:T(8,128)S(1)}, f32[1,1,128,16]{2,3,1,0:T(8,128)S(1)}, u32[]{:S(2)}, u32[]{:S(2)}) collective-permute-start(f32[1,1,128,16]{2,3,1,0:T(8,128)S(1)} %bitcast.295), channel_id=1, source_target_pairs={{0,40},{8,48},{16,56},{24,64},{32,72},{40,80},{48,88},{56,96},{64,... | collective-permute-start | bytes 24584 | tf_op jit(solution)/shard_map/ppermute | solution.py:26
  623.4 23.9 %collective-permute-start.62 = (f32[1,1,128,16]{2,3,1,0:T(8,128)S(1)}, f32[1,1,128,16]{2,3,1,0:T(8,128)S(1)}, u32[]{:S(2)}, u32[]{:S(2)}) collective-permute-start(f32[1,1,128,16]{2,3,1,0:T(8,128)S(1)} %bitcast.288), channel_id=1, source_target_pairs={{0,32},{8,40},{16,48},{24,56},{32,64},{40,72},{48,80},{56,88},{64,... | collective-permute-start | bytes 24584 | tf_op jit(solution)/shard_map/ppermute | solution.py:26
  625.7 23.0 %collective-permute-start.63 = (f32[1,1,128,16]{2,3,1,0:T(8,128)S(1)}, f32[1,1,128,16]{2,3,1,0:T(8,128)S(1)}, u32[]{:S(2)}, u32[]{:S(2)}) collective-permute-start(f32[1,1,128,16]{2,3,1,0:T(8,128)S(1)} %bitcast.283), channel_id=1, source_target_pairs={{0,24},{8,32},{16,40},{24,48},{32,56},{40,64},{48,72},{56,80},{64,... | collective-permute-start | bytes 24584 | tf_op jit(solution)/shard_map/ppermute | solution.py:26
  627.8 22.4 %collective-permute-start.64 = (f32[1,1,128,16]{2,3,1,0:T(8,128)S(1)}, f32[1,1,128,16]{2,3,1,0:T(8,128)S(1)}, u32[]{:S(2)}, u32[]{:S(2)}) collective-permute-start(f32[1,1,128,16]{2,3,1,0:T(8,128)S(1)} %bitcast.279), channel_id=1, source_target_pairs={{0,16},{8,24},{16,32},{24,40},{32,48},{40,56},{48,64},{56,72},{64,... | collective-permute-start | bytes 24584 | tf_op jit(solution)/shard_map/ppermute | solution.py:26
  629.8 21.8 %collective-permute-start.65 = (f32[1,1,128,16]{2,3,1,0:T(8,128)S(1)}, f32[1,1,128,16]{2,3,1,0:T(8,128)S(1)}, u32[]{:S(2)}, u32[]{:S(2)}) collective-permute-start(f32[1,1,128,16]{2,3,1,0:T(8,128)S(1)} %bitcast.273), channel_id=1, source_target_pairs={{0,8},{8,16},{16,24},{24,32},{32,40},{40,48},{48,56},{56,64},{64,7... | collective-permute-start | bytes 24584 | tf_op jit(solution)/shard_map/ppermute | solution.py:26
  694.4 41.4 %collective-permute-start.66 = (f32[1,1,128,16]{2,3,1,0:T(8,128)S(1)}, f32[1,1,128,16]{2,3,1,0:T(8,128)S(1)}, u32[]{:S(2)}, u32[]{:S(2)}) collective-permute-start(f32[1,1,128,16]{2,3,1,0:T(8,128)S(1)} %bitcast.332), channel_id=1, source_target_pairs={{8,0},{16,8},{24,16},{32,24},{40,32},{48,40},{56,48},{64,56},{72,6... | collective-permute-start | bytes 24584 | tf_op jit(solution)/shard_map/ppermute | solution.py:26
  701.5 54.4 %collective-permute-start.67 = (f32[1,1,128,16]{2,3,1,0:T(8,128)S(1)}, f32[1,1,128,16]{2,3,1,0:T(8,128)S(1)}, u32[]{:S(2)}, u32[]{:S(2)}) collective-permute-start(f32[1,1,128,16]{2,3,1,0:T(8,128)S(1)} %bitcast.328), channel_id=1, source_target_pairs={{16,0},{24,8},{32,16},{40,24},{48,32},{56,40},{64,48},{72,56},{80,... | collective-permute-start | bytes 24584 | tf_op jit(solution)/shard_map/ppermute | solution.py:26
  707.9 57.7 %collective-permute-start.68 = (f32[1,1,128,16]{2,3,1,0:T(8,128)S(1)}, f32[1,1,128,16]{2,3,1,0:T(8,128)S(1)}, u32[]{:S(2)}, u32[]{:S(2)}) collective-permute-start(f32[1,1,128,16]{2,3,1,0:T(8,128)S(1)} %bitcast.326), channel_id=1, source_target_pairs={{24,0},{32,8},{40,16},{48,24},{56,32},{64,40},{72,48},{80,56},{88,... | collective-permute-start | bytes 24584 | tf_op jit(solution)/shard_map/ppermute | solution.py:26
  716.4 61.6 %collective-permute-start.69 = (f32[1,1,128,16]{2,3,1,0:T(8,128)S(1)}, f32[1,1,128,16]{2,3,1,0:T(8,128)S(1)}, u32[]{:S(2)}, u32[]{:S(2)}) collective-permute-start(f32[1,1,128,16]{2,3,1,0:T(8,128)S(1)} %bitcast.324), channel_id=1, source_target_pairs={{32,0},{40,8},{48,16},{56,24},{64,32},{72,40},{80,48},{88,56},{96,... | collective-permute-start | bytes 24584 | tf_op jit(solution)/shard_map/ppermute | solution.py:26
  725.4 62.7 %collective-permute-start.70 = (f32[1,1,128,16]{2,3,1,0:T(8,128)S(1)}, f32[1,1,128,16]{2,3,1,0:T(8,128)S(1)}, u32[]{:S(2)}, u32[]{:S(2)}) collective-permute-start(f32[1,1,128,16]{2,3,1,0:T(8,128)S(1)} %bitcast.322), channel_id=1, source_target_pairs={{40,0},{48,8},{56,16},{64,24},{72,32},{80,40},{88,48},{96,56},{104... | collective-permute-start | bytes 24584 | tf_op jit(solution)/shard_map/ppermute | solution.py:26
  735.8 54.4 %collective-permute-start.71 = (f32[1,1,128,16]{2,3,1,0:T(8,128)S(1)}, f32[1,1,128,16]{2,3,1,0:T(8,128)S(1)}, u32[]{:S(2)}, u32[]{:S(2)}) collective-permute-start(f32[1,1,128,16]{2,3,1,0:T(8,128)S(1)} %bitcast.320), channel_id=1, source_target_pairs={{48,0},{56,8},{64,16},{72,24},{80,32},{88,40},{96,48},{104,56},{11... | collective-permute-start | bytes 24584 | tf_op jit(solution)/shard_map/ppermute | solution.py:26
  755.9 42.0 %collective-permute-start.72 = (f32[1,1,128,16]{2,3,1,0:T(8,128)S(1)}, f32[1,1,128,16]{2,3,1,0:T(8,128)S(1)}, u32[]{:S(2)}, u32[]{:S(2)}) collective-permute-start(f32[1,1,128,16]{2,3,1,0:T(8,128)S(1)} %bitcast.311), channel_id=1, source_target_pairs={{56,0},{64,8},{72,16},{80,24},{88,32},{96,40},{104,48},{112,56},{1... | collective-permute-start | bytes 24584 | tf_op jit(solution)/shard_map/ppermute | solution.py:26
  765.6 34.2 %collective-permute-start.73 = (f32[1,1,128,16]{2,3,1,0:T(8,128)S(1)}, f32[1,1,128,16]{2,3,1,0:T(8,128)S(1)}, u32[]{:S(2)}, u32[]{:S(2)}) collective-permute-start(f32[1,1,128,16]{2,3,1,0:T(8,128)S(1)} %bitcast.304), channel_id=1, source_target_pairs={{64,0},{72,8},{80,16},{88,24},{96,32},{104,40},{112,48},{120,56},{... | collective-permute-start | bytes 24584 | tf_op jit(solution)/shard_map/ppermute | solution.py:26
  778.0 23.8 %collective-permute-start.74 = (f32[1,1,128,16]{2,3,1,0:T(8,128)S(1)}, f32[1,1,128,16]{2,3,1,0:T(8,128)S(1)}, u32[]{:S(2)}, u32[]{:S(2)}) collective-permute-start(f32[1,1,128,16]{2,3,1,0:T(8,128)S(1)} %bitcast.299), channel_id=1, source_target_pairs={{72,0},{80,8},{88,16},{96,24},{104,32},{112,40},{120,48},{128,56},... | collective-permute-start | bytes 24584 | tf_op jit(solution)/shard_map/ppermute | solution.py:26
  797.9 22.0 %collective-permute-start.77 = (f32[1,1,128,16]{2,3,1,0:T(8,128)S(1)}, f32[1,1,128,16]{2,3,1,0:T(8,128)S(1)}, u32[]{:S(2)}, u32[]{:S(2)}) collective-permute-start(f32[1,1,128,16]{2,3,1,0:T(8,128)S(1)} %bitcast.291), channel_id=1, source_target_pairs={{96,0},{104,8},{112,16},{120,24},{128,32},{136,40},{144,48},{152,5... | collective-permute-start | bytes 24584 | tf_op jit(solution)/shard_map/ppermute | solution.py:26
  799.9 21.5 %collective-permute-start.78 = (f32[1,1,128,16]{2,3,1,0:T(8,128)S(1)}, f32[1,1,128,16]{2,3,1,0:T(8,128)S(1)}, u32[]{:S(2)}, u32[]{:S(2)}) collective-permute-start(f32[1,1,128,16]{2,3,1,0:T(8,128)S(1)} %bitcast.284), channel_id=1, source_target_pairs={{104,0},{112,8},{120,16},{128,24},{136,32},{144,40},{152,48},{160,... | collective-permute-start | bytes 24584 | tf_op jit(solution)/shard_map/ppermute | solution.py:26
  801.8 21.0 %collective-permute-start.79 = (f32[1,1,128,16]{2,3,1,0:T(8,128)S(1)}, f32[1,1,128,16]{2,3,1,0:T(8,128)S(1)}, u32[]{:S(2)}, u32[]{:S(2)}) collective-permute-start(f32[1,1,128,16]{2,3,1,0:T(8,128)S(1)} %bitcast.280), channel_id=1, source_target_pairs={{112,0},{120,8},{128,16},{136,24},{144,32},{152,40},{160,48},{168,... | collective-permute-start | bytes 24584 | tf_op jit(solution)/shard_map/ppermute | solution.py:26
  803.7 20.5 %collective-permute-start.80 = (f32[1,1,128,16]{2,3,1,0:T(8,128)S(1)}, f32[1,1,128,16]{2,3,1,0:T(8,128)S(1)}, u32[]{:S(2)}, u32[]{:S(2)}) collective-permute-start(f32[1,1,128,16]{2,3,1,0:T(8,128)S(1)} %bitcast.275), channel_id=1, source_target_pairs={{120,0},{128,8},{136,16},{144,24},{152,32},{160,40},{168,48},{176,... | collective-permute-start | bytes 24584 | tf_op jit(solution)/shard_map/ppermute | solution.py:26
  805.7 19.9 %collective-permute-start.81 = (f32[1,1,128,16]{2,3,1,0:T(8,128)S(1)}, f32[1,1,128,16]{2,3,1,0:T(8,128)S(1)}, u32[]{:S(2)}, u32[]{:S(2)}) collective-permute-start(f32[1,1,128,16]{2,3,1,0:T(8,128)S(1)} %bitcast.270), channel_id=1, source_target_pairs={{128,0},{136,8},{144,16},{152,24},{160,32},{168,40},{176,48},{184,... | collective-permute-start | bytes 24584 | tf_op jit(solution)/shard_map/ppermute | solution.py:26
  (21 other events, 350.7 us)
where the time goes:
time: 895 us; the launch traced here: 880 us
  local copies, waits for them, and re-layouts  449 us (50%)
  starting transfers between devices  380 us (42%)
  waiting for transfers between devices  20.2 us (2%)
  other arithmetic  14.6 us (2%)
  blocking collectives  14.6 us (2%)
    ppermute x70, starting transfers between devices, from_behind(): return lax.ppermute(shard, axis, pairs)  358 us
    unnamed x77, local copies, waits for them, and re-layouts  144 us
    dynamic_slice x76, local copies, waits for them, and re-layouts, piece_for(): return lax.dynamic_index_in_dim(tile_blocks, target, axis=1, keepdims=False)  142 us
    another operation x74, local copies, waits for them, and re-layouts, relayout(): window = jnp.stack(received[::-1], axis=0)  136 us
    dynamic_update_slice x2, local copies, waits for them, and re-layouts, relayout(): padded = lax.dynamic_update_slice_in_dim(padded, window, device_index, 0)  21.2 us
  transfers between devices with their start and end apart: 83, of which 8 were waited for; matrix products, arithmetic and copies ran while one was open for 28% of the time, Pallas kernels for 0%

commit v1 on v0

--- a/solution.py
+++ b/solution.py
@@ -4,6 +4,23 @@
 from jax.sharding import PartitionSpec as P
 
 STEPS = 3
+
+
+def tracks_launch(xs, dim_at, mat):
+    reply = xs.shape
+    front = jnp.moveaxis(
+        xs.reshape(*reply[:dim_at], mat, reply[dim_at] // mat, *reply[dim_at + 1 :]), dim_at, 0
+    )
+    return front
+
+
+def recover_quarters(inner_x, k_dim):
+    inner_x = jnp.moveaxis(inner_x, 0, k_dim)
+    long_array = inner_x.shape
+    e_now = inner_x.reshape(
+        *long_array[:k_dim], long_array[k_dim] * long_array[k_dim + 1], *long_array[k_dim + 2 :]
+    )
+    return e_now
 
 
 def extended_2(block, sides, width):
@@ -55,7 +72,16 @@
 def relayout(block, reach_rows):
     row_count = block.shape[0]
     lat_count = block.shape[1]
-    swapped = lax.all_to_all(block, "lon", split_axis=3, concat_axis=2, tiled=True)
+    local_now, prior = (lax.axis_size("lon"), lax.axis_index("lon"))
+    local_out = tracks_launch(block, 3, local_now)
+    xs_all = [local_out[prior]]
+    for tick in range(1, local_now):
+        piece_out = local_out[prior ^ tick]
+        xs_all.append(
+            lax.ppermute(piece_out, "lon", [(hop_no, hop_no ^ tick) for hop_no in range(local_now)])
+        )
+    local_out = jnp.stack(xs_all, 0)[prior ^ jnp.arange(local_now)]
+    swapped = recover_quarters(local_out, 2)
     lon_count = swapped.shape[2]
     col_count = swapped.shape[3]
     block_count = lat_count // row_count

time: 895 us -> 1000 us (1.12)
  starting transfers between devices: 380 us -> 584 us
  local copies, waits for them, and re-layouts: 449 us -> 371 us
  blocking collectives: 14.6 us -> 0 us
    ppermute x0 -> x14, starting transfers between devices: none -> 203 us  [relayout(): lax.ppermute(piece_out, 'lon', [(hop_no, hop_no ^ tick) for hop_no in ran...]
    unnamed x77 -> x55, local copies, waits for them, and re-layouts: 144 us -> 76.8 us
    all_to_all x1 -> x0, blocking collectives: 14.6 us -> none  [relayout(): lax.all_to_all(block, 'lon', split_axis=3, concat_axis=2, tiled=True)]
    dynamic_update_slice x2, local copies, waits for them, and re-layouts: 21.2 us -> 7.18 us  [relayout(): padded = lax.dynamic_update_slice_in_dim(padded, window, device_index, 0)]
    ppermute x0 -> x14, waiting for transfers between devices: none -> 11.8 us  [relayout(): lax.ppermute(piece_out, 'lon', [(hop_no, hop_no ^ tick) for hop_no in ran...]
    all_to_all x1 -> x0, waiting for transfers between devices: 10.3 us -> none  [relayout(): lax.all_to_all(block, 'lon', split_axis=3, concat_axis=2, tiled=True)]
    dynamic_slice x76 -> x75, local copies, waits for them, and re-layouts: 142 us -> 143 us  [piece_for(): return lax.dynamic_index_in_dim(tile_blocks, target, axis=1, keepdims=False)]
    another operation x74 -> x73, local copies, waits for them, and re-layouts: 136 us -> 138 us  [relayout(): window = jnp.stack(received[::-1], axis=0)]
  transfers between devices with their start and end apart: 83 -> 96, of which waited for: 8 -> 8; matrix products, arithmetic and copies ran while one was open for 28% -> 22% of each run, Pallas kernels for 0% -> 0%
where the time goes in v1:
time: 1000 us; the launch traced here: 988 us
  starting transfers between devices  584 us (58%)
  local copies, waits for them, and re-layouts  371 us (37%)
  waiting for transfers between devices  20.5 us (2%)
  other arithmetic  10.2 us (1%)
    ppermute x70, starting transfers between devices, from_behind(): return lax.ppermute(shard, axis, pairs)  363 us
    ppermute x14, starting transfers between devices, relayout(): lax.ppermute(piece_out, 'lon', [(hop_no, hop_no ^ tick) for hop_no in ran...  203 us
    dynamic_slice x75, local copies, waits for them, and re-layouts, piece_for(): return lax.dynamic_index_in_dim(tile_blocks, target, axis=1, keepdims=False)  143 us
    another operation x73, local copies, waits for them, and re-layouts, relayout(): window = jnp.stack(received[::-1], axis=0)  138 us
    unnamed x55, local copies, waits for them, and re-layouts  76.8 us
  transfers between devices with their start and end apart: 96, of which 8 were waited for; matrix products, arithmetic and copies ran while one was open for 22% of the time, Pallas kernels for 0%

profile of v1, /device:TPU:24, one launch (start us, length us, event | category | flops | bytes accessed | tf_op | source)
XLA Modules:
  0.0 987.6 jit_solution(14506343784714071860)
XLA Ops:
  2.2 2.9 collective-permute-start.1
  9.1 2.6 collective-permute-start.3
  15.3 3.0 collective-permute-start.5
  25.7 22.2 %collective-permute-start.8 = (f32[1,64,16,16]{1,3,2,0:T(8,128)S(1)}, f32[1,64,16,16]{1,3,2,0:T(8,128)S(1)}, u32[]{:S(2)}, u32[]{:S(2)}) collective-permute-start(f32[1,64,16,16]{1,3,2,0:T(8,128)S(1)} %get-tuple-element.100), channel_id=1, source_target_pairs={{0,3},{1,2},{2,1},{3,0},{4,7},{5,6},{6,5},{7,4},{8,11},{9,10},{10,... | collective-permute-start | bytes 196616 | tf_op jit(solution)/shard_map/ppermute | solution.py:81
  48.0 19.0 %collective-permute-start.9 = (f32[1,64,16,16]{1,3,2,0:T(8,128)S(1)}, f32[1,64,16,16]{1,3,2,0:T(8,128)S(1)}, u32[]{:S(2)}, u32[]{:S(2)}) collective-permute-start(f32[1,64,16,16]{1,3,2,0:T(8,128)S(1)} %get-tuple-element.99), channel_id=1, source_target_pairs={{0,4},{1,5},{2,6},{3,7},{4,0},{5,1},{6,2},{7,3},{8,12},{9,13},{10,... | collective-permute-start | bytes 196616 | tf_op jit(solution)/shard_map/ppermute | solution.py:81
  67.0 19.0 %collective-permute-start.10 = (f32[1,64,16,16]{1,3,2,0:T(8,128)S(1)}, f32[1,64,16,16]{1,3,2,0:T(8,128)S(1)}, u32[]{:S(2)}, u32[]{:S(2)}) collective-permute-start(f32[1,64,16,16]{1,3,2,0:T(8,128)S(1)} %get-tuple-element.98), channel_id=1, source_target_pairs={{0,5},{1,4},{2,7},{3,6},{4,1},{5,0},{6,3},{7,2},{8,13},{9,12},{10,... | collective-permute-start | bytes 196616 | tf_op jit(solution)/shard_map/ppermute | solution.py:81
  86.0 19.0 %collective-permute-start.11 = (f32[1,64,16,16]{1,3,2,0:T(8,128)S(1)}, f32[1,64,16,16]{1,3,2,0:T(8,128)S(1)}, u32[]{:S(2)}, u32[]{:S(2)}) collective-permute-start(f32[1,64,16,16]{1,3,2,0:T(8,128)S(1)} %get-tuple-element.97), channel_id=1, source_target_pairs={{0,6},{1,7},{2,4},{3,5},{4,2},{5,3},{6,0},{7,1},{8,14},{9,15},{10,... | collective-permute-start | bytes 196616 | tf_op jit(solution)/shard_map/ppermute | solution.py:81
  105.1 19.0 %collective-permute-start.12 = (f32[1,64,16,16]{1,3,2,0:T(8,128)S(1)}, f32[1,64,16,16]{1,3,2,0:T(8,128)S(1)}, u32[]{:S(2)}, u32[]{:S(2)}) collective-permute-start(f32[1,64,16,16]{1,3,2,0:T(8,128)S(1)} %get-tuple-element.96), channel_id=1, source_target_pairs={{0,7},{1,6},{2,5},{3,4},{4,3},{5,2},{6,1},{7,0},{8,15},{9,14},{10,... | collective-permute-start | bytes 196616 | tf_op jit(solution)/shard_map/ppermute | solution.py:81
  124.2 5.9 collective-permute-done.12
  130.8 8.4 constant_dynamic-slice_fusion.32
  140.8 9.5 collective-permute-start.33
  151.9 5.6 collective-permute-start.34
  159.1 4.1 collective-permute-start.35
  168.4 9.1 collective-permute-start.37
  182.4 5.6 collective-permute-start.38
  188.1 8.2 collective-permute-start.39
  196.3 4.3 collective-permute-start.40
  227.5 11.2 %collective-permute-start.48 = (f32[1,1,128,16]{2,3,1,0:T(8,128)S(1)}, f32[1,1,128,16]{2,3,1,0:T(8,128)S(1)}, u32[]{:S(2)}, u32[]{:S(2)}) collective-permute-start(f32[1,1,128,16]{2,3,1,0:T(8,128)S(1)} %bitcast.325), channel_id=1, source_target_pairs={{136,0},{144,8},{152,16},{160,24},{168,32},{176,40},{184,48},{192,... | collective-permute-start | bytes 24584 | tf_op jit(solution)/shard_map/ppermute | solution.py:43
  238.8 19.0 %collective-permute-start.49 = (f32[1,1,128,16]{2,3,1,0:T(8,128)S(1)}, f32[1,1,128,16]{2,3,1,0:T(8,128)S(1)}, u32[]{:S(2)}, u32[]{:S(2)}) collective-permute-start(f32[1,1,128,16]{2,3,1,0:T(8,128)S(1)} %bitcast.319), channel_id=1, source_target_pairs={{144,0},{152,8},{160,16},{168,24},{176,32},{184,40},{192,48},{200,... | collective-permute-start | bytes 24584 | tf_op jit(solution)/shard_map/ppermute | solution.py:43
  257.8 19.0 %collective-permute-start.50 = (f32[1,1,128,16]{2,3,1,0:T(8,128)S(1)}, f32[1,1,128,16]{2,3,1,0:T(8,128)S(1)}, u32[]{:S(2)}, u32[]{:S(2)}) collective-permute-start(f32[1,1,128,16]{2,3,1,0:T(8,128)S(1)} %bitcast.316), channel_id=1, source_target_pairs={{152,0},{160,8},{168,16},{176,24},{184,32},{192,40},{200,48},{208,... | collective-permute-start | bytes 24584 | tf_op jit(solution)/shard_map/ppermute | solution.py:43
  276.9 8.4 constant_dynamic-slice_fusion.50
  294.7 8.6 collective-permute-start.17
  317.3 3.1 collective-permute-start.21
  326.3 4.8 collective-permute-start.25
  348.6 2.5 collective-permute-start.29
  353.0 2.6 constant_dynamic-slice_fusion.68
  362.5 2.5 collective-permute-start.31
  365.0 5.5 collective-permute-start.32
  370.5 35.0 %collective-permute-start.13 = (f32[1,1,128,16]{2,3,1,0:T(8,128)S(1)}, f32[1,1,128,16]{2,3,1,0:T(8,128)}, u32[]{:S(2)}, u32[]{:S(2)}) collective-permute-start(f32[1,1,128,16]{2,3,1,0:T(8,128)S(1)} %bitcast.303), channel_id=1, source_target_pairs={{0,152},{8,160},{16,168},{24,176},{32,184},{40,192},{48,200},{56,2... | collective-permute-start | bytes 24584 | tf_op jit(solution)/shard_map/ppermute | solution.py:43
  405.5 19.0 %collective-permute-start.14 = (f32[1,1,128,16]{2,3,1,0:T(8,128)S(1)}, f32[1,1,128,16]{2,3,1,0:T(8,128)}, u32[]{:S(2)}, u32[]{:S(2)}) collective-permute-start(f32[1,1,128,16]{2,3,1,0:T(8,128)S(1)} %bitcast.299), channel_id=1, source_target_pairs={{0,144},{8,152},{16,160},{24,168},{32,176},{40,184},{48,192},{56,2... | collective-permute-start | bytes 24584 | tf_op jit(solution)/shard_map/ppermute | solution.py:43
  424.5 19.0 %collective-permute-start.15 = (f32[1,1,128,16]{2,3,1,0:T(8,128)S(1)}, f32[1,1,128,16]{2,3,1,0:T(8,128)}, u32[]{:S(2)}, u32[]{:S(2)}) collective-permute-start(f32[1,1,128,16]{2,3,1,0:T(8,128)S(1)} %bitcast.297), channel_id=1, source_target_pairs={{0,136},{8,144},{16,152},{24,160},{32,168},{40,176},{48,184},{56,1... | collective-permute-start | bytes 24584 | tf_op jit(solution)/shard_map/ppermute | solution.py:43
  444.6 12.1 %copy.525 = f32[1,1,1,128,16]{0,3,4,2,1:T(8,128)S(1)} copy(f32[1,1,1,128,16]{1,4,3,2,0:T(8,128)S(1)} %get-tuple-element.76) | data formatting | bytes 16384
  509.8 23.2 %stack.312 = f32[39,1,1,128,16]{0,3,4,2,1:T(8,128)} concatenate(f32[1,1,1,128,16]{0,3,4,2,1:T(8,128)} %copy.422, f32[1,1,1,128,16]{0,3,4,2,1:T(8,128)} %copy.423, f32[1,1,1,128,16]{0,3,4,2,1:T(8,128)} %copy.424, f32[1,1,1,128,16]{0,3,4,2,1:T(8,128)} %copy.425, f32[1,1,1,128,16]{0,3,4,2,1:T(8,128)} %copy.426, f32[1,1,1,128,16]{0,3,4,2,1:T(8,128)} %copy.427, ...), dimensions={0} | concatenate | bytes 638976 | tf_op jit(solution)/shard_map/stack | solution.py:103
  533.1 7.2 dynamic_update_slice.6
  540.8 2.8 collective-permute-start.52
  546.9 2.6 collective-permute-start.54
  552.4 3.0 collective-permute-start.56
  562.2 21.5 %collective-permute-start.59 = (f32[1,64,16,16]{1,3,2,0:T(8,128)S(1)}, f32[1,64,16,16]{1,3,2,0:T(8,128)S(1)}, u32[]{:S(2)}, u32[]{:S(2)}) collective-permute-start(f32[1,64,16,16]{1,3,2,0:T(8,128)S(1)} %get-tuple-element.42), channel_id=1, source_target_pairs={{0,3},{1,2},{2,1},{3,0},{4,7},{5,6},{6,5},{7,4},{8,11},{9,10},{10,... | collective-permute-start | bytes 196616 | tf_op jit(solution)/shard_map/ppermute | solution.py:81
  583.6 19.0 %collective-permute-start.60 = (f32[1,64,16,16]{1,3,2,0:T(8,128)S(1)}, f32[1,64,16,16]{1,3,2,0:T(8,128)S(1)}, u32[]{:S(2)}, u32[]{:S(2)}) collective-permute-start(f32[1,64,16,16]{1,3,2,0:T(8,128)S(1)} %get-tuple-element.41), channel_id=1, source_target_pairs={{0,4},{1,5},{2,6},{3,7},{4,0},{5,1},{6,2},{7,3},{8,12},{9,13},{10,... | collective-permute-start | bytes 196616 | tf_op jit(solution)/shard_map/ppermute | solution.py:81
  602.7 19.0 %collective-permute-start.61 = (f32[1,64,16,16]{1,3,2,0:T(8,128)S(1)}, f32[1,64,16,16]{1,3,2,0:T(8,128)S(1)}, u32[]{:S(2)}, u32[]{:S(2)}) collective-permute-start(f32[1,64,16,16]{1,3,2,0:T(8,128)S(1)} %get-tuple-element.40), channel_id=1, source_target_pairs={{0,5},{1,4},{2,7},{3,6},{4,1},{5,0},{6,3},{7,2},{8,13},{9,12},{10,... | collective-permute-start | bytes 196616 | tf_op jit(solution)/shard_map/ppermute | solution.py:81
  621.7 19.0 %collective-permute-start.62 = (f32[1,64,16,16]{1,3,2,0:T(8,128)S(1)}, f32[1,64,16,16]{1,3,2,0:T(8,128)S(1)}, u32[]{:S(2)}, u32[]{:S(2)}) collective-permute-start(f32[1,64,16,16]{1,3,2,0:T(8,128)S(1)} %get-tuple-element.39), channel_id=1, source_target_pairs={{0,6},{1,7},{2,4},{3,5},{4,2},{5,3},{6,0},{7,1},{8,14},{9,15},{10,... | collective-permute-start | bytes 196616 | tf_op jit(solution)/shard_map/ppermute | solution.py:81
  640.7 19.0 %collective-permute-start.63 = (f32[1,64,16,16]{1,3,2,0:T(8,128)S(1)}, f32[1,64,16,16]{1,3,2,0:T(8,128)S(1)}, u32[]{:S(2)}, u32[]{:S(2)}) collective-permute-start(f32[1,64,16,16]{1,3,2,0:T(8,128)S(1)} %get-tuple-element.38), channel_id=1, source_target_pairs={{0,7},{1,6},{2,5},{3,4},{4,3},{5,2},{6,1},{7,0},{8,15},{9,14},{10,... | collective-permute-start | bytes 196616 | tf_op jit(solution)/shard_map/ppermute | solution.py:81
  659.9 5.9 collective-permute-done.63
  666.6 7.4 constant_dynamic-slice_fusion.16
  678.6 8.6 collective-permute-start.65
  699.5 3.1 collective-permute-start.69
  716.6 4.4 collective-permute-start.73
  733.1 2.5 collective-permute-start.77
  737.5 2.9 collective-permute-start.79
  772.4 2.3 constant_dynamic-update-slice_fusion.25
  785.9 2.3 constant_dynamic-update-slice_fusion.18
  790.4 2.3 constant_dynamic-update-slice_fusion.16
  792.7 7.8 constant_dynamic-slice_fusion
  802.2 5.5 collective-permute-start.80
  809.3 4.8 collective-permute-start.81
  815.7 6.4 collective-permute-start.82
  823.7 7.8 collective-permute-start.83
  833.2 8.7 collective-permute-start.84
  843.5 11.9 %collective-permute-start.85 = (f32[1,1,128,16]{2,3,1,0:T(8,128)S(1)}, f32[1,1,128,16]{2,3,1,0:T(8,128)S(1)}, u32[]{:S(2)}, u32[]{:S(2)}) collective-permute-start(f32[1,1,128,16]{2,3,1,0:T(8,128)S(1)} %bitcast.376), channel_id=1, source_target_pairs={{48,0},{56,8},{64,16},{72,24},{80,32},{88,40},{96,48},{104,56},{11... | collective-permute-start | bytes 24584 | tf_op jit(solution)/shard_map/ppermute | solution.py:43
  863.6 9.7 collective-permute-start.86
  873.3 12.4 %collective-permute-start.87 = (f32[1,1,128,16]{2,3,1,0:T(8,128)S(1)}, f32[1,1,128,16]{2,3,1,0:T(8,128)S(1)}, u32[]{:S(2)}, u32[]{:S(2)}) collective-permute-start(f32[1,1,128,16]{2,3,1,0:T(8,128)S(1)} %bitcast.357), channel_id=1, source_target_pairs={{64,0},{72,8},{80,16},{88,24},{96,32},{104,40},{112,48},{120,56},{... | collective-permute-start | bytes 24584 | tf_op jit(solution)/shard_map/ppermute | solution.py:43
  885.7 10.1 %collective-permute-start.88 = (f32[1,1,128,16]{2,3,1,0:T(8,128)S(1)}, f32[1,1,128,16]{2,3,1,0:T(8,128)S(1)}, u32[]{:S(2)}, u32[]{:S(2)}) collective-permute-start(f32[1,1,128,16]{2,3,1,0:T(8,128)S(1)} %bitcast.353), channel_id=1, source_target_pairs={{72,0},{80,8},{88,16},{96,24},{104,32},{112,40},{120,48},{128,56},... | collective-permute-start | bytes 24584 | tf_op jit(solution)/shard_map/ppermute | solution.py:43
  946.1 2.3 constant_dynamic-update-slice_fusion.10
  967.5 19.0 %copy.524 = f32[33,1,1,128,16]{3,4,0,2,1:T(8,128)S(1)} copy(f32[33,1,1,128,16]{1,4,3,2,0:T(8,128)} %constant_dynamic-update-slice_fusion) | data formatting | bytes 540672 | tf_op jit(solution)/shard_map/stack | solution.py:103
  (368 shorter events, 361.6 us)
Async XLA Ops:
  21.9 64.2 %collective-permute-start.6 = (f32[1,64,16,16]{1,3,2,0:T(8,128)S(1)}, f32[1,64,16,16]{1,3,2,0:T(8,128)S(1)}, u32[]{:S(2)}, u32[]{:S(2)}) collective-permute-start(f32[1,64,16,16]{1,3,2,0:T(8,128)S(1)} %get-tuple-element.102), channel_id=1, source_target_pairs={{0,1},{1,0},{2,3},{3,2},{4,5},{5,4},{6,7},{7,6},{8,9},{9,8},{10,11... | collective-permute-start | bytes 196616 | tf_op jit(solution)/shard_map/ppermute | solution.py:81
  23.8 81.3 %collective-permute-start.7 = (f32[1,64,16,16]{1,3,2,0:T(8,128)S(1)}, f32[1,64,16,16]{1,3,2,0:T(8,128)S(1)}, u32[]{:S(2)}, u32[]{:S(2)}) collective-permute-start(f32[1,64,16,16]{1,3,2,0:T(8,128)S(1)} %get-tuple-element.101), channel_id=1, source_target_pairs={{0,2},{1,3},{2,0},{3,1},{4,6},{5,7},{6,4},{7,5},{8,10},{9,11},{10,... | collective-permute-start | bytes 196616 | tf_op jit(solution)/shard_map/ppermute | solution.py:81
  25.7 98.4 %collective-permute-start.8 = (f32[1,64,16,16]{1,3,2,0:T(8,128)S(1)}, f32[1,64,16,16]{1,3,2,0:T(8,128)S(1)}, u32[]{:S(2)}, u32[]{:S(2)}) collective-permute-start(f32[1,64,16,16]{1,3,2,0:T(8,128)S(1)} %get-tuple-element.100), channel_id=1, source_target_pairs={{0,3},{1,2},{2,1},{3,0},{4,7},{5,6},{6,5},{7,4},{8,11},{9,10},{10,... | collective-permute-start | bytes 196616 | tf_op jit(solution)/shard_map/ppermute | solution.py:81
  48.0 76.2 %collective-permute-start.9 = (f32[1,64,16,16]{1,3,2,0:T(8,128)S(1)}, f32[1,64,16,16]{1,3,2,0:T(8,128)S(1)}, u32[]{:S(2)}, u32[]{:S(2)}) collective-permute-start(f32[1,64,16,16]{1,3,2,0:T(8,128)S(1)} %get-tuple-element.99), channel_id=1, source_target_pairs={{0,4},{1,5},{2,6},{3,7},{4,0},{5,1},{6,2},{7,3},{8,12},{9,13},{10,... | collective-permute-start | bytes 196616 | tf_op jit(solution)/shard_map/ppermute | solution.py:81
  67.0 57.2 %collective-permute-start.10 = (f32[1,64,16,16]{1,3,2,0:T(8,128)S(1)}, f32[1,64,16,16]{1,3,2,0:T(8,128)S(1)}, u32[]{:S(2)}, u32[]{:S(2)}) collective-permute-start(f32[1,64,16,16]{1,3,2,0:T(8,128)S(1)} %get-tuple-element.98), channel_id=1, source_target_pairs={{0,5},{1,4},{2,7},{3,6},{4,1},{5,0},{6,3},{7,2},{8,13},{9,12},{10,... | collective-permute-start | bytes 196616 | tf_op jit(solution)/shard_map/ppermute | solution.py:81
  86.0 38.2 %collective-permute-start.11 = (f32[1,64,16,16]{1,3,2,0:T(8,128)S(1)}, f32[1,64,16,16]{1,3,2,0:T(8,128)S(1)}, u32[]{:S(2)}, u32[]{:S(2)}) collective-permute-start(f32[1,64,16,16]{1,3,2,0:T(8,128)S(1)} %get-tuple-element.97), channel_id=1, source_target_pairs={{0,6},{1,7},{2,4},{3,5},{4,2},{5,3},{6,0},{7,1},{8,14},{9,15},{10,... | collective-permute-start | bytes 196616 | tf_op jit(solution)/shard_map/ppermute | solution.py:81
  105.1 25.0 %collective-permute-start.12 = (f32[1,64,16,16]{1,3,2,0:T(8,128)S(1)}, f32[1,64,16,16]{1,3,2,0:T(8,128)S(1)}, u32[]{:S(2)}, u32[]{:S(2)}) collective-permute-start(f32[1,64,16,16]{1,3,2,0:T(8,128)S(1)} %get-tuple-element.96), channel_id=1, source_target_pairs={{0,7},{1,6},{2,5},{3,4},{4,3},{5,2},{6,1},{7,0},{8,15},{9,14},{10,... | collective-permute-start | bytes 196616 | tf_op jit(solution)/shard_map/ppermute | solution.py:81
  140.8 41.6 %collective-permute-start.33 = (f32[1,1,128,16]{2,3,1,0:T(8,128)S(1)}, f32[1,1,128,16]{2,3,1,0:T(8,128)S(1)}, u32[]{:S(2)}, u32[]{:S(2)}) collective-permute-start(f32[1,1,128,16]{2,3,1,0:T(8,128)S(1)} %bitcast.387), channel_id=1, source_target_pairs={{16,0},{24,8},{32,16},{40,24},{48,32},{56,40},{64,48},{72,56},{80,... | collective-permute-start | bytes 24584 | tf_op jit(solution)/shard_map/ppermute | solution.py:43
  151.9 36.1 %collective-permute-start.34 = (f32[1,1,128,16]{2,3,1,0:T(8,128)S(1)}, f32[1,1,128,16]{2,3,1,0:T(8,128)S(1)}, u32[]{:S(2)}, u32[]{:S(2)}) collective-permute-start(f32[1,1,128,16]{2,3,1,0:T(8,128)S(1)} %bitcast.386), channel_id=1, source_target_pairs={{24,0},{32,8},{40,16},{48,24},{56,32},{64,40},{72,48},{80,56},{88,... | collective-permute-start | bytes 24584 | tf_op jit(solution)/shard_map/ppermute | solution.py:43
  159.1 37.2 %collective-permute-start.35 = (f32[1,1,128,16]{2,3,1,0:T(8,128)S(1)}, f32[1,1,128,16]{2,3,1,0:T(8,128)S(1)}, u32[]{:S(2)}, u32[]{:S(2)}) collective-permute-start(f32[1,1,128,16]{2,3,1,0:T(8,128)S(1)} %bitcast.385), channel_id=1, source_target_pairs={{32,0},{40,8},{48,16},{56,24},{64,32},{72,40},{80,48},{88,56},{96,... | collective-permute-start | bytes 24584 | tf_op jit(solution)/shard_map/ppermute | solution.py:43
  164.9 44.0 %collective-permute-start.36 = (f32[1,1,128,16]{2,3,1,0:T(8,128)S(1)}, f32[1,1,128,16]{2,3,1,0:T(8,128)S(1)}, u32[]{:S(2)}, u32[]{:S(2)}) collective-permute-start(f32[1,1,128,16]{2,3,1,0:T(8,128)S(1)} %bitcast.373), channel_id=1, source_target_pairs={{40,0},{48,8},{56,16},{64,24},{72,32},{80,40},{88,48},{96,56},{104... | collective-permute-start | bytes 24584 | tf_op jit(solution)/shard_map/ppermute | solution.py:43
  168.4 42.3 %collective-permute-start.37 = (f32[1,1,128,16]{2,3,1,0:T(8,128)S(1)}, f32[1,1,128,16]{2,3,1,0:T(8,128)S(1)}, u32[]{:S(2)}, u32[]{:S(2)}) collective-permute-start(f32[1,1,128,16]{2,3,1,0:T(8,128)S(1)} %bitcast.371), channel_id=1, source_target_pairs={{48,0},{56,8},{64,16},{72,24},{80,32},{88,40},{96,48},{104,56},{11... | collective-permute-start | bytes 24584 | tf_op jit(solution)/shard_map/ppermute | solution.py:43
  182.4 30.3 %collective-permute-start.38 = (f32[1,1,128,16]{2,3,1,0:T(8,128)S(1)}, f32[1,1,128,16]{2,3,1,0:T(8,128)S(1)}, u32[]{:S(2)}, u32[]{:S(2)}) collective-permute-start(f32[1,1,128,16]{2,3,1,0:T(8,128)S(1)} %bitcast.369), channel_id=1, source_target_pairs={{56,0},{64,8},{72,16},{80,24},{88,32},{96,40},{104,48},{112,56},{1... | collective-permute-start | bytes 24584 | tf_op jit(solution)/shard_map/ppermute | solution.py:43
  188.1 26.5 %collective-permute-start.39 = (f32[1,1,128,16]{2,3,1,0:T(8,128)S(1)}, f32[1,1,128,16]{2,3,1,0:T(8,128)S(1)}, u32[]{:S(2)}, u32[]{:S(2)}) collective-permute-start(f32[1,1,128,16]{2,3,1,0:T(8,128)S(1)} %bitcast.361), channel_id=1, source_target_pairs={{64,0},{72,8},{80,16},{88,24},{96,32},{104,40},{112,48},{120,56},{... | collective-permute-start | bytes 24584 | tf_op jit(solution)/shard_map/ppermute | solution.py:43
  214.6 24.2 %collective-permute-start.44 = (f32[1,1,128,16]{2,3,1,0:T(8,128)S(1)}, f32[1,1,128,16]{2,3,1,0:T(8,128)S(1)}, u32[]{:S(2)}, u32[]{:S(2)}) collective-permute-start(f32[1,1,128,16]{2,3,1,0:T(8,128)S(1)} %bitcast.289), channel_id=1, source_target_pairs={{104,0},{112,8},{120,16},{128,24},{136,32},{144,40},{152,48},{160,... | collective-permute-start | bytes 24584 | tf_op jit(solution)/shard_map/ppermute | solution.py:43
  216.6 41.3 %collective-permute-start.45 = (f32[1,1,128,16]{2,3,1,0:T(8,128)S(1)}, f32[1,1,128,16]{2,3,1,0:T(8,128)S(1)}, u32[]{:S(2)}, u32[]{:S(2)}) collective-permute-start(f32[1,1,128,16]{2,3,1,0:T(8,128)S(1)} %bitcast.288), channel_id=1, source_target_pairs={{112,0},{120,8},{128,16},{136,24},{144,32},{152,40},{160,48},{168,... | collective-permute-start | bytes 24584 | tf_op jit(solution)/shard_map/ppermute | solution.py:43
  224.3 69.1 %collective-permute-start.46 = (f32[1,1,128,16]{2,3,1,0:T(8,128)S(1)}, f32[1,1,128,16]{2,3,1,0:T(8,128)S(1)}, u32[]{:S(2)}, u32[]{:S(2)}) collective-permute-start(f32[1,1,128,16]{2,3,1,0:T(8,128)S(1)} %bitcast.343), channel_id=1, source_target_pairs={{120,0},{128,8},{136,16},{144,24},{152,32},{160,40},{168,48},{176,... | collective-permute-start | bytes 24584 | tf_op jit(solution)/shard_map/ppermute | solution.py:43
  226.2 68.5 %collective-permute-start.47 = (f32[1,1,128,16]{2,3,1,0:T(8,128)S(1)}, f32[1,1,128,16]{2,3,1,0:T(8,128)S(1)}, u32[]{:S(2)}, u32[]{:S(2)}) collective-permute-start(f32[1,1,128,16]{2,3,1,0:T(8,128)S(1)} %bitcast.333), channel_id=1, source_target_pairs={{128,0},{136,8},{144,16},{152,24},{160,32},{168,40},{176,48},{184,... | collective-permute-start | bytes 24584 | tf_op jit(solution)/shard_map/ppermute | solution.py:43
  227.5 75.8 %collective-permute-start.48 = (f32[1,1,128,16]{2,3,1,0:T(8,128)S(1)}, f32[1,1,128,16]{2,3,1,0:T(8,128)S(1)}, u32[]{:S(2)}, u32[]{:S(2)}) collective-permute-start(f32[1,1,128,16]{2,3,1,0:T(8,128)S(1)} %bitcast.325), channel_id=1, source_target_pairs={{136,0},{144,8},{152,16},{160,24},{168,32},{176,40},{184,48},{192,... | collective-permute-start | bytes 24584 | tf_op jit(solution)/shard_map/ppermute | solution.py:43
  238.8 66.5 %collective-permute-start.49 = (f32[1,1,128,16]{2,3,1,0:T(8,128)S(1)}, f32[1,1,128,16]{2,3,1,0:T(8,128)S(1)}, u32[]{:S(2)}, u32[]{:S(2)}) collective-permute-start(f32[1,1,128,16]{2,3,1,0:T(8,128)S(1)} %bitcast.319), channel_id=1, source_target_pairs={{144,0},{152,8},{160,16},{168,24},{176,32},{184,40},{192,48},{200,... | collective-permute-start | bytes 24584 | tf_op jit(solution)/shard_map/ppermute | solution.py:43
  257.8 49.4 %collective-permute-start.50 = (f32[1,1,128,16]{2,3,1,0:T(8,128)S(1)}, f32[1,1,128,16]{2,3,1,0:T(8,128)S(1)}, u32[]{:S(2)}, u32[]{:S(2)}) collective-permute-start(f32[1,1,128,16]{2,3,1,0:T(8,128)S(1)} %bitcast.316), channel_id=1, source_target_pairs={{152,0},{160,8},{168,16},{176,24},{184,32},{192,40},{200,48},{208,... | collective-permute-start | bytes 24584 | tf_op jit(solution)/shard_map/ppermute | solution.py:43
  293.4 23.9 %collective-permute-start.16 = (f32[1,1,128,16]{2,3,1,0:T(8,128)S(1)}, f32[1,1,128,16]{2,3,1,0:T(8,128)S(1)}, u32[]{:S(2)}, u32[]{:S(2)}) collective-permute-start(f32[1,1,128,16]{2,3,1,0:T(8,128)S(1)} %bitcast.363), channel_id=1, source_target_pairs={{0,128},{8,136},{16,144},{24,152},{32,160},{40,168},{48,176},{56,1... | collective-permute-start | bytes 24584 | tf_op jit(solution)/shard_map/ppermute | solution.py:43
  294.7 25.7 %collective-permute-start.17 = (f32[1,1,128,16]{2,3,1,0:T(8,128)S(1)}, f32[1,1,128,16]{2,3,1,0:T(8,128)S(1)}, u32[]{:S(2)}, u32[]{:S(2)}) collective-permute-start(f32[1,1,128,16]{2,3,1,0:T(8,128)S(1)} %bitcast.356), channel_id=1, source_target_pairs={{0,120},{8,128},{16,136},{24,144},{32,152},{40,160},{48,168},{56,1... | collective-permute-start | bytes 24584 | tf_op jit(solution)/shard_map/ppermute | solution.py:43
  317.3 25.4 %collective-permute-start.21 = (f32[1,1,128,16]{2,3,1,0:T(8,128)S(1)}, f32[1,1,128,16]{2,3,1,0:T(8,128)S(1)}, u32[]{:S(2)}, u32[]{:S(2)}) collective-permute-start(f32[1,1,128,16]{2,3,1,0:T(8,128)S(1)} %bitcast.334), channel_id=1, source_target_pairs={{0,88},{8,96},{16,104},{24,112},{32,120},{40,128},{48,136},{56,144... | collective-permute-start | bytes 24584 | tf_op jit(solution)/shard_map/ppermute | solution.py:43
  320.5 24.2 %collective-permute-start.22 = (f32[1,1,128,16]{2,3,1,0:T(8,128)S(1)}, f32[1,1,128,16]{2,3,1,0:T(8,128)S(1)}, u32[]{:S(2)}, u32[]{:S(2)}) collective-permute-start(f32[1,1,128,16]{2,3,1,0:T(8,128)S(1)} %bitcast.326), channel_id=1, source_target_pairs={{0,80},{8,88},{16,96},{24,104},{32,112},{40,120},{48,128},{56,136}... | collective-permute-start | bytes 24584 | tf_op jit(solution)/shard_map/ppermute | solution.py:43
  322.4 24.2 %collective-permute-start.23 = (f32[1,1,128,16]{2,3,1,0:T(8,128)S(1)}, f32[1,1,128,16]{2,3,1,0:T(8,128)S(1)}, u32[]{:S(2)}, u32[]{:S(2)}) collective-permute-start(f32[1,1,128,16]{2,3,1,0:T(8,128)S(1)} %bitcast.320), channel_id=1, source_target_pairs={{0,72},{8,80},{16,88},{24,96},{32,104},{40,112},{48,120},{56,128},... | collective-permute-start | bytes 24584 | tf_op jit(solution)/shard_map/ppermute | solution.py:43
  324.3 24.2 %collective-permute-start.24 = (f32[1,1,128,16]{2,3,1,0:T(8,128)S(1)}, f32[1,1,128,16]{2,3,1,0:T(8,128)S(1)}, u32[]{:S(2)}, u32[]{:S(2)}) collective-permute-start(f32[1,1,128,16]{2,3,1,0:T(8,128)S(1)} %bitcast.315), channel_id=1, source_target_pairs={{0,64},{8,72},{16,80},{24,88},{32,96},{40,104},{48,112},{56,120},{... | collective-permute-start | bytes 24584 | tf_op jit(solution)/shard_map/ppermute | solution.py:43
  326.3 24.8 %collective-permute-start.25 = (f32[1,1,128,16]{2,3,1,0:T(8,128)S(1)}, f32[1,1,128,16]{2,3,1,0:T(8,128)S(1)}, u32[]{:S(2)}, u32[]{:S(2)}) collective-permute-start(f32[1,1,128,16]{2,3,1,0:T(8,128)S(1)} %bitcast.314), channel_id=1, source_target_pairs={{0,56},{8,64},{16,72},{24,80},{32,88},{40,96},{48,104},{56,112},{6... | collective-permute-start | bytes 24584 | tf_op jit(solution)/shard_map/ppermute | solution.py:43
  346.6 23.9 %collective-permute-start.28 = (f32[1,1,128,16]{2,3,1,0:T(8,128)}, f32[1,1,128,16]{2,3,1,0:T(8,128)S(1)}, u32[]{:S(2)}, u32[]{:S(2)}) collective-permute-start(f32[1,1,128,16]{2,3,1,0:T(8,128)} %bitcast.66), channel_id=1, source_target_pairs={{0,32},{8,40},{16,48},{24,56},{32,64},{40,72},{48,80},{56,88},{64,... | collective-permute-start | bytes 24584 | tf_op jit(solution)/shard_map/ppermute | solution.py:43
  348.6 56.9 %collective-permute-start.29 = (f32[1,1,128,16]{2,3,1,0:T(8,128)}, f32[1,1,128,16]{2,3,1,0:T(8,128)S(1)}, u32[]{:S(2)}, u32[]{:S(2)}) collective-permute-start(f32[1,1,128,16]{2,3,1,0:T(8,128)} %bitcast.68), channel_id=1, source_target_pairs={{0,24},{8,32},{16,40},{24,48},{32,56},{40,64},{48,72},{56,80},{64,... | collective-permute-start | bytes 24584 | tf_op jit(solution)/shard_map/ppermute | solution.py:43
  351.0 73.5 %collective-permute-start.30 = (f32[1,1,128,16]{2,3,1,0:T(8,128)}, f32[1,1,128,16]{2,3,1,0:T(8,128)S(1)}, u32[]{:S(2)}, u32[]{:S(2)}) collective-permute-start(f32[1,1,128,16]{2,3,1,0:T(8,128)} %bitcast.70), channel_id=1, source_target_pairs={{0,16},{8,24},{16,32},{24,40},{32,48},{40,56},{48,64},{56,72},{64,... | collective-permute-start | bytes 24584 | tf_op jit(solution)/shard_map/ppermute | solution.py:43
  362.5 137.0 %collective-permute-start.31 = (f32[1,1,128,16]{2,3,1,0:T(8,128)S(1)}, f32[1,1,128,16]{2,3,1,0:T(8,128)}, u32[]{:S(2)}, u32[]{:S(2)}) collective-permute-start(f32[1,1,128,16]{2,3,1,0:T(8,128)S(1)} %bitcast.309), channel_id=1, source_target_pairs={{0,8},{8,16},{16,24},{24,32},{32,40},{40,48},{48,56},{56,64},{64,7... | collective-permute-start | bytes 24584 | tf_op jit(solution)/shard_map/ppermute | solution.py:43
  365.0 136.6 %collective-permute-start.32 = (f32[1,1,128,16]{2,3,1,0:T(8,128)S(1)}, f32[1,1,128,16]{2,3,1,0:T(8,128)}, u32[]{:S(2)}, u32[]{:S(2)}) collective-permute-start(f32[1,1,128,16]{2,3,1,0:T(8,128)S(1)} %bitcast.306), channel_id=1, source_target_pairs={{8,0},{16,8},{24,16},{32,24},{40,32},{48,40},{56,48},{64,56},{72,6... | collective-permute-start | bytes 24584 | tf_op jit(solution)/shard_map/ppermute | solution.py:43
  370.5 133.2 %collective-permute-start.13 = (f32[1,1,128,16]{2,3,1,0:T(8,128)S(1)}, f32[1,1,128,16]{2,3,1,0:T(8,128)}, u32[]{:S(2)}, u32[]{:S(2)}) collective-permute-start(f32[1,1,128,16]{2,3,1,0:T(8,128)S(1)} %bitcast.303), channel_id=1, source_target_pairs={{0,152},{8,160},{16,168},{24,176},{32,184},{40,192},{48,200},{56,2... | collective-permute-start | bytes 24584 | tf_op jit(solution)/shard_map/ppermute | solution.py:43
  405.5 100.2 %collective-permute-start.14 = (f32[1,1,128,16]{2,3,1,0:T(8,128)S(1)}, f32[1,1,128,16]{2,3,1,0:T(8,128)}, u32[]{:S(2)}, u32[]{:S(2)}) collective-permute-start(f32[1,1,128,16]{2,3,1,0:T(8,128)S(1)} %bitcast.299), channel_id=1, source_target_pairs={{0,144},{8,152},{16,160},{24,168},{32,176},{40,184},{48,192},{56,2... | collective-permute-start | bytes 24584 | tf_op jit(solution)/shard_map/ppermute | solution.py:43
  424.5 83.3 %collective-permute-start.15 = (f32[1,1,128,16]{2,3,1,0:T(8,128)S(1)}, f32[1,1,128,16]{2,3,1,0:T(8,128)}, u32[]{:S(2)}, u32[]{:S(2)}) collective-permute-start(f32[1,1,128,16]{2,3,1,0:T(8,128)S(1)} %bitcast.297), channel_id=1, source_target_pairs={{0,136},{8,144},{16,152},{24,160},{32,168},{40,176},{48,184},{56,1... | collective-permute-start | bytes 24584 | tf_op jit(solution)/shard_map/ppermute | solution.py:43
  558.3 63.4 %collective-permute-start.57 = (f32[1,64,16,16]{1,3,2,0:T(8,128)S(1)}, f32[1,64,16,16]{1,3,2,0:T(8,128)S(1)}, u32[]{:S(2)}, u32[]{:S(2)}) collective-permute-start(f32[1,64,16,16]{1,3,2,0:T(8,128)S(1)} %get-tuple-element.44), channel_id=1, source_target_pairs={{0,1},{1,0},{2,3},{3,2},{4,5},{5,4},{6,7},{7,6},{8,9},{9,8},{10,11... | collective-permute-start | bytes 196616 | tf_op jit(solution)/shard_map/ppermute | solution.py:81
  560.2 80.5 %collective-permute-start.58 = (f32[1,64,16,16]{1,3,2,0:T(8,128)S(1)}, f32[1,64,16,16]{1,3,2,0:T(8,128)S(1)}, u32[]{:S(2)}, u32[]{:S(2)}) collective-permute-start(f32[1,64,16,16]{1,3,2,0:T(8,128)S(1)} %get-tuple-element.43), channel_id=1, source_target_pairs={{0,2},{1,3},{2,0},{3,1},{4,6},{5,7},{6,4},{7,5},{8,10},{9,11},{10,... | collective-permute-start | bytes 196616 | tf_op jit(solution)/shard_map/ppermute | solution.py:81
  562.2 97.6 %collective-permute-start.59 = (f32[1,64,16,16]{1,3,2,0:T(8,128)S(1)}, f32[1,64,16,16]{1,3,2,0:T(8,128)S(1)}, u32[]{:S(2)}, u32[]{:S(2)}) collective-permute-start(f32[1,64,16,16]{1,3,2,0:T(8,128)S(1)} %get-tuple-element.42), channel_id=1, source_target_pairs={{0,3},{1,2},{2,1},{3,0},{4,7},{5,6},{6,5},{7,4},{8,11},{9,10},{10,... | collective-permute-start | bytes 196616 | tf_op jit(solution)/shard_map/ppermute | solution.py:81
  583.6 76.2 %collective-permute-start.60 = (f32[1,64,16,16]{1,3,2,0:T(8,128)S(1)}, f32[1,64,16,16]{1,3,2,0:T(8,128)S(1)}, u32[]{:S(2)}, u32[]{:S(2)}) collective-permute-start(f32[1,64,16,16]{1,3,2,0:T(8,128)S(1)} %get-tuple-element.41), channel_id=1, source_target_pairs={{0,4},{1,5},{2,6},{3,7},{4,0},{5,1},{6,2},{7,3},{8,12},{9,13},{10,... | collective-permute-start | bytes 196616 | tf_op jit(solution)/shard_map/ppermute | solution.py:81
  602.7 57.2 %collective-permute-start.61 = (f32[1,64,16,16]{1,3,2,0:T(8,128)S(1)}, f32[1,64,16,16]{1,3,2,0:T(8,128)S(1)}, u32[]{:S(2)}, u32[]{:S(2)}) collective-permute-start(f32[1,64,16,16]{1,3,2,0:T(8,128)S(1)} %get-tuple-element.40), channel_id=1, source_target_pairs={{0,5},{1,4},{2,7},{3,6},{4,1},{5,0},{6,3},{7,2},{8,13},{9,12},{10,... | collective-permute-start | bytes 196616 | tf_op jit(solution)/shard_map/ppermute | solution.py:81
  621.7 38.2 %collective-permute-start.62 = (f32[1,64,16,16]{1,3,2,0:T(8,128)S(1)}, f32[1,64,16,16]{1,3,2,0:T(8,128)S(1)}, u32[]{:S(2)}, u32[]{:S(2)}) collective-permute-start(f32[1,64,16,16]{1,3,2,0:T(8,128)S(1)} %get-tuple-element.39), channel_id=1, source_target_pairs={{0,6},{1,7},{2,4},{3,5},{4,2},{5,3},{6,0},{7,1},{8,14},{9,15},{10,... | collective-permute-start | bytes 196616 | tf_op jit(solution)/shard_map/ppermute | solution.py:81
  640.7 25.0 %collective-permute-start.63 = (f32[1,64,16,16]{1,3,2,0:T(8,128)S(1)}, f32[1,64,16,16]{1,3,2,0:T(8,128)S(1)}, u32[]{:S(2)}, u32[]{:S(2)}) collective-permute-start(f32[1,64,16,16]{1,3,2,0:T(8,128)S(1)} %get-tuple-element.38), channel_id=1, source_target_pairs={{0,7},{1,6},{2,5},{3,4},{4,3},{5,2},{6,1},{7,0},{8,15},{9,14},{10,... | collective-permute-start | bytes 196616 | tf_op jit(solution)/shard_map/ppermute | solution.py:81
  675.6 23.8 %collective-permute-start.64 = (f32[1,1,128,16]{2,3,1,0:T(8,128)S(1)}, f32[1,1,128,16]{2,3,1,0:T(8,128)S(1)}, u32[]{:S(2)}, u32[]{:S(2)}) collective-permute-start(f32[1,1,128,16]{2,3,1,0:T(8,128)S(1)} %bitcast.388), channel_id=1, source_target_pairs={{0,128},{8,136},{16,144},{24,152},{32,160},{40,168},{48,176},{56,1... | collective-permute-start | bytes 24584 | tf_op jit(solution)/shard_map/ppermute | solution.py:43
  678.6 32.2 %collective-permute-start.65 = (f32[1,1,128,16]{2,3,1,0:T(8,128)S(1)}, f32[1,1,128,16]{2,3,1,0:T(8,128)S(1)}, u32[]{:S(2)}, u32[]{:S(2)}) collective-permute-start(f32[1,1,128,16]{2,3,1,0:T(8,128)S(1)} %bitcast.383), channel_id=1, source_target_pairs={{0,120},{8,128},{16,136},{24,144},{32,152},{40,160},{48,168},{56,1... | collective-permute-start | bytes 24584 | tf_op jit(solution)/shard_map/ppermute | solution.py:43
  688.8 23.9 %collective-permute-start.66 = (f32[1,1,128,16]{2,3,1,0:T(8,128)S(1)}, f32[1,1,128,16]{2,3,1,0:T(8,128)S(1)}, u32[]{:S(2)}, u32[]{:S(2)}) collective-permute-start(f32[1,1,128,16]{2,3,1,0:T(8,128)S(1)} %bitcast.381), channel_id=1, source_target_pairs={{0,112},{8,120},{16,128},{24,136},{32,144},{40,152},{48,160},{56,1... | collective-permute-start | bytes 24584 | tf_op jit(solution)/shard_map/ppermute | solution.py:43
  692.4 22.3 %collective-permute-start.67 = (f32[1,1,128,16]{2,3,1,0:T(8,128)S(1)}, f32[1,1,128,16]{2,3,1,0:T(8,128)S(1)}, u32[]{:S(2)}, u32[]{:S(2)}) collective-permute-start(f32[1,1,128,16]{2,3,1,0:T(8,128)S(1)} %bitcast.379), channel_id=1, source_target_pairs={{0,104},{8,112},{16,120},{24,128},{32,136},{40,144},{48,152},{56,1... | collective-permute-start | bytes 24584 | tf_op jit(solution)/shard_map/ppermute | solution.py:43
  699.5 21.5 %collective-permute-start.69 = (f32[1,1,128,16]{2,3,1,0:T(8,128)S(1)}, f32[1,1,128,16]{2,3,1,0:T(8,128)S(1)}, u32[]{:S(2)}, u32[]{:S(2)}) collective-permute-start(f32[1,1,128,16]{2,3,1,0:T(8,128)S(1)} %bitcast.374), channel_id=1, source_target_pairs={{0,88},{8,96},{16,104},{24,112},{32,120},{40,128},{48,136},{56,144... | collective-permute-start | bytes 24584 | tf_op jit(solution)/shard_map/ppermute | solution.py:43
  729.2 24.7 %collective-permute-start.75 = (f32[1,1,128,16]{2,3,1,0:T(8,128)S(1)}, f32[1,1,128,16]{2,3,1,0:T(8,128)S(1)}, u32[]{:S(2)}, u32[]{:S(2)}) collective-permute-start(f32[1,1,128,16]{2,3,1,0:T(8,128)S(1)} %bitcast.351), channel_id=1, source_target_pairs={{0,40},{8,48},{16,56},{24,64},{32,72},{40,80},{48,88},{56,96},{64,... | collective-permute-start | bytes 24584 | tf_op jit(solution)/shard_map/ppermute | solution.py:43
  731.1 24.2 %collective-permute-start.76 = (f32[1,1,128,16]{2,3,1,0:T(8,128)S(1)}, f32[1,1,128,16]{2,3,1,0:T(8,128)S(1)}, u32[]{:S(2)}, u32[]{:S(2)}) collective-permute-start(f32[1,1,128,16]{2,3,1,0:T(8,128)S(1)} %bitcast.344), channel_id=1, source_target_pairs={{0,32},{8,40},{16,48},{24,56},{32,64},{40,72},{48,80},{56,88},{64,... | collective-permute-start | bytes 24584 | tf_op jit(solution)/shard_map/ppermute | solution.py:43
  733.1 23.7 %collective-permute-start.77 = (f32[1,1,128,16]{2,3,1,0:T(8,128)S(1)}, f32[1,1,128,16]{2,3,1,0:T(8,128)S(1)}, u32[]{:S(2)}, u32[]{:S(2)}) collective-permute-start(f32[1,1,128,16]{2,3,1,0:T(8,128)S(1)} %bitcast.339), channel_id=1, source_target_pairs={{0,24},{8,32},{16,40},{24,48},{32,56},{40,64},{48,72},{56,80},{64,... | collective-permute-start | bytes 24584 | tf_op jit(solution)/shard_map/ppermute | solution.py:43
  735.6 22.6 %collective-permute-start.78 = (f32[1,1,128,16]{2,3,1,0:T(8,128)S(1)}, f32[1,1,128,16]{2,3,1,0:T(8,128)S(1)}, u32[]{:S(2)}, u32[]{:S(2)}) collective-permute-start(f32[1,1,128,16]{2,3,1,0:T(8,128)S(1)} %bitcast.332), channel_id=1, source_target_pairs={{0,16},{8,24},{16,32},{24,40},{32,48},{40,56},{48,64},{56,72},{64,... | collective-permute-start | bytes 24584 | tf_op jit(solution)/shard_map/ppermute | solution.py:43
  737.5 22.1 %collective-permute-start.79 = (f32[1,1,128,16]{2,3,1,0:T(8,128)S(1)}, f32[1,1,128,16]{2,3,1,0:T(8,128)S(1)}, u32[]{:S(2)}, u32[]{:S(2)}) collective-permute-start(f32[1,1,128,16]{2,3,1,0:T(8,128)S(1)} %bitcast.327), channel_id=1, source_target_pairs={{0,8},{8,16},{16,24},{24,32},{32,40},{40,48},{48,56},{56,64},{64,7... | collective-permute-start | bytes 24584 | tf_op jit(solution)/shard_map/ppermute | solution.py:43
  802.2 41.4 %collective-permute-start.80 = (f32[1,1,128,16]{2,3,1,0:T(8,128)S(1)}, f32[1,1,128,16]{2,3,1,0:T(8,128)S(1)}, u32[]{:S(2)}, u32[]{:S(2)}) collective-permute-start(f32[1,1,128,16]{2,3,1,0:T(8,128)S(1)} %bitcast.389), channel_id=1, source_target_pairs={{8,0},{16,8},{24,16},{32,24},{40,32},{48,40},{56,48},{64,56},{72,6... | collective-permute-start | bytes 24584 | tf_op jit(solution)/shard_map/ppermute | solution.py:43
  809.3 54.3 %collective-permute-start.81 = (f32[1,1,128,16]{2,3,1,0:T(8,128)S(1)}, f32[1,1,128,16]{2,3,1,0:T(8,128)S(1)}, u32[]{:S(2)}, u32[]{:S(2)}) collective-permute-start(f32[1,1,128,16]{2,3,1,0:T(8,128)S(1)} %bitcast.384), channel_id=1, source_target_pairs={{16,0},{24,8},{32,16},{40,24},{48,32},{56,40},{64,48},{72,56},{80,... | collective-permute-start | bytes 24584 | tf_op jit(solution)/shard_map/ppermute | solution.py:43
  815.7 57.6 %collective-permute-start.82 = (f32[1,1,128,16]{2,3,1,0:T(8,128)S(1)}, f32[1,1,128,16]{2,3,1,0:T(8,128)S(1)}, u32[]{:S(2)}, u32[]{:S(2)}) collective-permute-start(f32[1,1,128,16]{2,3,1,0:T(8,128)S(1)} %bitcast.382), channel_id=1, source_target_pairs={{24,0},{32,8},{40,16},{48,24},{56,32},{64,40},{72,48},{80,56},{88,... | collective-permute-start | bytes 24584 | tf_op jit(solution)/shard_map/ppermute | solution.py:43
  823.7 62.0 %collective-permute-start.83 = (f32[1,1,128,16]{2,3,1,0:T(8,128)S(1)}, f32[1,1,128,16]{2,3,1,0:T(8,128)S(1)}, u32[]{:S(2)}, u32[]{:S(2)}) collective-permute-start(f32[1,1,128,16]{2,3,1,0:T(8,128)S(1)} %bitcast.380), channel_id=1, source_target_pairs={{32,0},{40,8},{48,16},{56,24},{64,32},{72,40},{80,48},{88,56},{96,... | collective-permute-start | bytes 24584 | tf_op jit(solution)/shard_map/ppermute | solution.py:43
  833.2 62.6 %collective-permute-start.84 = (f32[1,1,128,16]{2,3,1,0:T(8,128)S(1)}, f32[1,1,128,16]{2,3,1,0:T(8,128)S(1)}, u32[]{:S(2)}, u32[]{:S(2)}) collective-permute-start(f32[1,1,128,16]{2,3,1,0:T(8,128)S(1)} %bitcast.378), channel_id=1, source_target_pairs={{40,0},{48,8},{56,16},{64,24},{72,32},{80,40},{88,48},{96,56},{104... | collective-permute-start | bytes 24584 | tf_op jit(solution)/shard_map/ppermute | solution.py:43
  843.5 54.4 %collective-permute-start.85 = (f32[1,1,128,16]{2,3,1,0:T(8,128)S(1)}, f32[1,1,128,16]{2,3,1,0:T(8,128)S(1)}, u32[]{:S(2)}, u32[]{:S(2)}) collective-permute-start(f32[1,1,128,16]{2,3,1,0:T(8,128)S(1)} %bitcast.376), channel_id=1, source_target_pairs={{48,0},{56,8},{64,16},{72,24},{80,32},{88,40},{96,48},{104,56},{11... | collective-permute-start | bytes 24584 | tf_op jit(solution)/shard_map/ppermute | solution.py:43
  863.6 42.0 %collective-permute-start.86 = (f32[1,1,128,16]{2,3,1,0:T(8,128)S(1)}, f32[1,1,128,16]{2,3,1,0:T(8,128)S(1)}, u32[]{:S(2)}, u32[]{:S(2)}) collective-permute-start(f32[1,1,128,16]{2,3,1,0:T(8,128)S(1)} %bitcast.365), channel_id=1, source_target_pairs={{56,0},{64,8},{72,16},{80,24},{88,32},{96,40},{104,48},{112,56},{1... | collective-permute-start | bytes 24584 | tf_op jit(solution)/shard_map/ppermute | solution.py:43
  873.3 34.2 %collective-permute-start.87 = (f32[1,1,128,16]{2,3,1,0:T(8,128)S(1)}, f32[1,1,128,16]{2,3,1,0:T(8,128)S(1)}, u32[]{:S(2)}, u32[]{:S(2)}) collective-permute-start(f32[1,1,128,16]{2,3,1,0:T(8,128)S(1)} %bitcast.357), channel_id=1, source_target_pairs={{64,0},{72,8},{80,16},{88,24},{96,32},{104,40},{112,48},{120,56},{... | collective-permute-start | bytes 24584 | tf_op jit(solution)/shard_map/ppermute | solution.py:43
  885.7 23.8 %collective-permute-start.88 = (f32[1,1,128,16]{2,3,1,0:T(8,128)S(1)}, f32[1,1,128,16]{2,3,1,0:T(8,128)S(1)}, u32[]{:S(2)}, u32[]{:S(2)}) collective-permute-start(f32[1,1,128,16]{2,3,1,0:T(8,128)S(1)} %bitcast.353), channel_id=1, source_target_pairs={{72,0},{80,8},{88,16},{96,24},{104,32},{112,40},{120,48},{128,56},... | collective-permute-start | bytes 24584 | tf_op jit(solution)/shard_map/ppermute | solution.py:43
  905.6 22.1 %collective-permute-start.91 = (f32[1,1,128,16]{2,3,1,0:T(8,128)S(1)}, f32[1,1,128,16]{2,3,1,0:T(8,128)S(1)}, u32[]{:S(2)}, u32[]{:S(2)}) collective-permute-start(f32[1,1,128,16]{2,3,1,0:T(8,128)S(1)} %bitcast.348), channel_id=1, source_target_pairs={{96,0},{104,8},{112,16},{120,24},{128,32},{136,40},{144,48},{152,5... | collective-permute-start | bytes 24584 | tf_op jit(solution)/shard_map/ppermute | solution.py:43
  907.6 21.5 %collective-permute-start.92 = (f32[1,1,128,16]{2,3,1,0:T(8,128)S(1)}, f32[1,1,128,16]{2,3,1,0:T(8,128)S(1)}, u32[]{:S(2)}, u32[]{:S(2)}) collective-permute-start(f32[1,1,128,16]{2,3,1,0:T(8,128)S(1)} %bitcast.340), channel_id=1, source_target_pairs={{104,0},{112,8},{120,16},{128,24},{136,32},{144,40},{152,48},{160,... | collective-permute-start | bytes 24584 | tf_op jit(solution)/shard_map/ppermute | solution.py:43
  (36 other events, 859.9 us)
